TPU v7x, 32 devices: a whole 2x2x4 slice. The times are simulated.
32 devices in a mesh: row: 16 (over z, y, core), col: 2 (over x).
Axes of the slice: x: 2, y: 2, z: 4, core: 2. Of those that a mesh axis runs over, the one named last changes fastest.
Arguments:
- crop: bfloat16 [256, 256, 512], P('row', 'col'), may hold values from -6 to 6
- tissue: int32 [16, 16], P('row', 'col'), may hold values 0 or 1
- w_qkv: bfloat16 [512, 1536], replicated, may hold values from -0.25 to 0.25
- w_proj: bfloat16 [512, 512], replicated, may hold values from -0.25 to 0.25
- w_fc1: bfloat16 [512, 2048], replicated, may hold values from -0.25 to 0.25
- w_fc2: bfloat16 [2048, 512], replicated, may hold values from -0.125 to 0.125
- logit_scale: float32 [16], replicated, may hold values from 1.5 to 5.5
- bias_table: float32 [16, 31, 31], replicated, may hold values from 0 to 16
- norm1_gain: float32 [512], replicated, may hold values from 0.5 to 1.5
- norm1_bias: float32 [512], replicated, may hold values from -1 to 1
- norm2_gain: float32 [512], replicated, may hold values from 0.5 to 1.5
- norm2_bias: float32 [512], replicated, may hold values from -1 to 1
Outputs:
- block_out: bfloat16 [256, 256, 512], P('row', 'col')
All inputs are finite; a program needn't handle non-finite values. No bound on the sum of `tissue` on one device may be relied on, other than what follows from the above.
Results may differ from a plain program's by a relative error of at most 0.012.
The roundings to bfloat16 on the way count: a program that leaves them out, or rounds other values in their place, can miss the bound.
Values may be sent and summed in bfloat16 or wider, within the bound.
A program may use at most 192 MiB of HBM per device.

v0:
```python
import math

import jax
import jax.numpy as jnp
from jax import lax
from jax.sharding import PartitionSpec as P

DIM = 512
HEADS = 16
WIN = 16
HEAD_DIM = 32
SHIFT = 8


def shifted(x, axis, by):
    count = lax.axis_size(axis)
    return lax.ppermute(x, axis, [(i, (i + by) % count) for i in range(count)])


def full_bias(bias_table):
    places = jnp.arange(WIN, dtype=jnp.int32)
    offset_ids = jnp.arange(2 * WIN - 1, dtype=jnp.int32)
    select = (
        places[:, None, None] - places[None, :, None] + WIN - 1 == offset_ids[None, None, :]
    ).astype(jnp.float32)
    by_cols = jnp.einsum("uvb,hab->hauv", select, bias_table, precision=lax.Precision.HIGHEST)
    both = jnp.einsum("xya,hauv->hxuyv", select, by_cols, precision=lax.Precision.HIGHEST)
    return both.reshape(HEADS, WIN * WIN, WIN * WIN)


def region_label(coords, total):
    return jnp.where(coords < total - WIN, 0, jnp.where(coords < total - SHIFT, 1, 2)).astype(
        jnp.int32
    )


def layer_norm(values, gain, offset):
    centre = jnp.mean(values, axis=-1, keepdims=True)
    centred = values - centre
    spread = jnp.mean(centred * centred, axis=-1, keepdims=True)
    return centred * lax.rsqrt(spread + 1e-05) * gain + offset


def unit_rows(values):
    return values * lax.rsqrt(jnp.sum(values * values, axis=-1, keepdims=True) + 1e-06)


def attend_windows(tokens, labels, token_mask, params):
    w_qkv, w_proj, head_scale, bias, norm1_gain, norm1_bias = params
    count = tokens.shape[0]
    flat = tokens.reshape(count * WIN * WIN, DIM)
    triple = jnp.dot(flat, w_qkv, preferred_element_type=jnp.float32).astype(jnp.bfloat16)
    triple = triple.reshape(count, WIN * WIN, 3, HEADS, HEAD_DIM)
    query_unit = unit_rows(triple[:, :, 0].astype(jnp.float32)).astype(jnp.bfloat16)
    key_unit = unit_rows(triple[:, :, 1].astype(jnp.float32)).astype(jnp.bfloat16)
    values = triple[:, :, 2]
    scores = jnp.einsum("nqhd,nkhd->nhqk", query_unit, key_unit, preferred_element_type=jnp.float32)
    same = labels[:, :, None] == labels[:, None, :]
    penalty = jnp.where(same, jnp.float32(0.0), jnp.float32(-100.0))
    scores = scores * head_scale[None, :, None, None] + bias[None] + penalty[:, None]
    highest = jnp.max(scores, axis=-1, keepdims=True)
    raised = jnp.exp(scores - highest)
    weights = (raised / jnp.sum(raised, axis=-1, keepdims=True)).astype(jnp.bfloat16)
    mixed = jnp.einsum(
        "nhqk,nkhd->nqhd", weights, values, preferred_element_type=jnp.float32
    ).astype(jnp.bfloat16)
    projected = jnp.dot(
        mixed.reshape(count * WIN * WIN, DIM), w_proj, preferred_element_type=jnp.float32
    )
    branch = layer_norm(projected, norm1_gain, norm1_bias)
    result = flat.astype(jnp.float32) + token_mask.reshape(-1, 1) * branch
    return result.astype(jnp.bfloat16).reshape(count, WIN * WIN, DIM)


def feed_forward(tokens, token_mask, w_fc1, w_fc2, norm2_gain, norm2_bias):
    hidden = jax.nn.gelu(
        jnp.dot(tokens, w_fc1, preferred_element_type=jnp.float32), approximate=False
    ).astype(jnp.bfloat16)
    grown = jnp.dot(hidden, w_fc2, preferred_element_type=jnp.float32)
    return (
        tokens.astype(jnp.float32) + token_mask[:, None] * layer_norm(grown, norm2_gain, norm2_bias)
    ).astype(jnp.bfloat16)


def attend_region(region, window_flags, row_coords, col_coords, total_rows, total_cols, params):
    region_rows, region_cols = (region.shape[0], region.shape[1])
    win_rows = region_rows // WIN
    win_cols = region_cols // WIN
    windows = (
        region.reshape(win_rows, WIN, win_cols, WIN, DIM)
        .transpose(0, 2, 1, 3, 4)
        .reshape(win_rows, win_cols, WIN * WIN, DIM)
    )
    row_label = region_label(row_coords, total_rows).reshape(win_rows, WIN)
    col_label = region_label(col_coords, total_cols).reshape(win_cols, WIN)
    labels = (3 * row_label[:, None, :, None] + col_label[None, :, None, :]).reshape(
        win_rows, win_cols, WIN * WIN
    )
    flags = window_flags.astype(jnp.float32)

    def one_row(items):
        tokens, marks, row_flags = items
        token_mask = jnp.broadcast_to(row_flags[:, None], (win_cols, WIN * WIN))
        return attend_windows(tokens, marks, token_mask, params)

    mixed = lax.map(one_row, (windows, labels, flags))
    mixed = (
        mixed.reshape(win_rows, win_cols, WIN, WIN, DIM)
        .transpose(0, 2, 1, 3, 4)
        .reshape(region_rows, region_cols, DIM)
    )
    token_mask = jnp.broadcast_to(flags[:, None, :, None], (win_rows, WIN, win_cols, WIN)).reshape(
        region_rows, region_cols
    )
    return (mixed, token_mask)


def on_device(
    crop,
    tissue,
    w_qkv,
    w_proj,
    w_fc1,
    w_fc2,
    logit_scale,
    bias_table,
    norm1_gain,
    norm1_bias,
    norm2_gain,
    norm2_bias,
):
    tile_rows, tile_cols = (crop.shape[0], crop.shape[1])
    total_rows = tile_rows * lax.axis_size("row")
    total_cols = tile_cols * lax.axis_size("col")
    row_place = lax.axis_index("row")
    col_place = lax.axis_index("col")
    head_scale = jnp.exp(jnp.minimum(logit_scale, math.log(100.0)))
    params = (w_qkv, w_proj, head_scale, full_bias(bias_table), norm1_gain, norm1_bias)
    beside = shifted(crop[:, :SHIFT], "col", -1)
    widened = jnp.concatenate([crop[:, SHIFT:], beside], axis=1)
    below = shifted(widened[:SHIFT], "row", -1)
    rolled = jnp.concatenate([widened[SHIFT:], below], axis=0)
    row_coords = row_place * tile_rows + jnp.arange(tile_rows, dtype=jnp.int32)
    col_coords = col_place * tile_cols + jnp.arange(tile_cols, dtype=jnp.int32)
    mixed, token_mask = attend_region(
        rolled, tissue, row_coords, col_coords, total_rows, total_cols, params
    )
    finished = feed_forward(
        mixed.reshape(tile_rows * tile_cols, DIM),
        token_mask.reshape(-1),
        w_fc1,
        w_fc2,
        norm2_gain,
        norm2_bias,
    )
    finished = finished.reshape(tile_rows, tile_cols, DIM)
    above = shifted(finished[tile_rows - SHIFT :], "row", 1)
    lifted = jnp.concatenate([above, finished[: tile_rows - SHIFT]], axis=0)
    leftward = shifted(lifted[:, tile_cols - SHIFT :], "col", 1)
    return jnp.concatenate([leftward, lifted[:, : tile_cols - SHIFT]], axis=1)


def solution(mesh):
    in_specs = (
        P("row", "col", None),
        P("row", "col"),
        P(),
        P(),
        P(),
        P(),
        P(),
        P(),
        P(),
        P(),
        P(),
        P(),
    )
    out_specs = P("row", "col", None)
    return jax.shard_map(
        on_device, mesh=mesh, in_specs=in_specs, out_specs=out_specs, check_vma=False
    )
```

profile of v0, /device:TPU:0, one launch (start us, length us, event | category | flops | bytes accessed | tf_op | source)
XLA Modules:
  0.0 243.5 jit_solution(9952679348749842523)
XLA Ops:
  0.0 1.1 slice.43
  1.1 3.0 %collective-permute-start = (bf16[16,8,512]{2,1,0:T(8,128)(2,1)S(1)}, bf16[16,8,512]{2,1,0:T(8,128)(2,1)S(1)}, u32[]{:S(2)}, u32[]{:S(2)}) collective-permute-start(bf16[16,8,512]{2,1,0:T(8,128)(2,1)S(1)} %slice.43), channel_id=1, source_target_pairs={{0,1},{1,0},{2,3},{3,2},{4,5},{5,4},{6,7},{7,6},{8,9},{9,8},{10,11... | collective-permute-start | bytes 393224 | tf_op jit(solution)/shard_map/ppermute | solution.py:17
  4.1 3.0 %slice.42 = bf16[16,120,512]{2,1,0:T(8,128)(2,1)} slice(bf16[16,128,512]{2,1,0:T(8,128)(2,1)} %param.12), slice={[0:16], [8:128], [0:512]} | slice | bytes 3932160 | tf_op jit(solution)/shard_map/slice | solution.py:140
  7.1 0.1 add.169
  7.2 1.0 fusion.40
  8.2 0.0 copy-start.13
  8.2 17.4 %convolution_bitcast_fusion = f32[16,16,16,16,16]{3,4,1,2,0:T(8,128)} fusion(f32[16,16,16,31]{3,1,0,2:T(8,128)S(1)} %fusion.40, s32[16,16]{1,0:T(8,128)S(1)} %subtract_add_fusion), kind=kOutput, calls=%fused_computation.28 | convolution fusion | flops 390078208 | bytes 4703232 | tf_op jit(solution)/shard_map/xya,hauv->hxuyv/dot_general | solution.py:27
  25.7 2.7 %fusion.39 = (bf16[8,128,512]{2,1,0:T(8,128)(2,1)S(1)}, bf16[8,128,512]{2,1,0:T(8,128)(2,1)}) fusion(bf16[16,120,512]{2,1,0:T(8,128)(2,1)} %slice.42, bf16[16,8,512]{2,1,0:T(8,128)(2,1)S(1)} %collective-permute-done), kind=kLoop, calls=%fused_computation.61 | loop fusion | flops 4194304 | bytes 4194304 | tf_op jit(solution)/shard_map/concatenate | solution.py:140
  28.4 3.7 %collective-permute-start.1 = (bf16[8,128,512]{2,1,0:T(8,128)(2,1)}, bf16[8,128,512]{2,1,0:T(8,128)(2,1)}, u32[]{:S(2)}, u32[]{:S(2)}) collective-permute-start(bf16[8,128,512]{2,1,0:T(8,128)(2,1)} %get-tuple-element.32), channel_id=1, source_target_pairs={{0,30},{2,0},{4,2},{6,4},{8,6},{10,8},{12,10},{14,12},{16,14},{18,... | collective-permute-start | bytes 3145736 | tf_op jit(solution)/shard_map/ppermute | solution.py:17
  32.1 0.1 add.163
  32.2 0.1 add.164
  32.3 41.5 %copy.33 = f32[16,16,16,16,16]{2,1,4,3,0:T(8,128)} copy(f32[16,16,16,16,16]{3,4,1,2,0:T(8,128)} %convolution_bitcast_fusion) | data formatting | bytes 8388608 | tf_op jit(solution)/shard_map/while/body/eval_jaxpr/add | solution.py:60
  73.7 23.5 %reshape.177 = f32[16,256,256]{1,2,0:T(8,128)} reshape(f32[16,16,16,16,16]{2,1,4,3,0:T(8,128)} %copy.33) | data formatting | bytes 8388608 | tf_op jit(solution)/shard_map/while/body/eval_jaxpr/add | solution.py:60
  97.2 0.1 broadcast_bitcast_fusion
  97.3 0.1 broadcast_in_dim.99
  97.4 0.7 broadcast_in_dim.100
  98.0 1.7 compare_select_fusion
  99.7 1.5 pad_maximum_fusion.1
  101.2 0.2 copy.19
  101.4 1.3 copy-done.2
  102.8 5.2 %convolution_convert_fusion = bf16[2048,1536]{1,0:T(8,128)(2,1)} fusion(bf16[2048,512]{1,0:T(8,128)(2,1)S(1)} %bitcast.92, bf16[512,1536]{1,0:T(8,128)(2,1)S(1)} %copy-done.12), kind=kOutput, calls=%fused_computation.30 | convolution fusion | flops 3224371200 | bytes 9961472 | tf_op jit(solution)/shard_map/while/body/eval_jaxpr/dot_general | solution.py:52
  108.0 8.7 %copy.20 = bf16[2048,1536]{0,1:T(8,128)(2,1)} copy(bf16[2048,1536]{1,0:T(8,128)(2,1)} %convolution_convert_fusion) | data formatting | bytes 12582912 | tf_op jit(solution)/shard_map/while/body/eval_jaxpr/convert_element_type | solution.py:52
  116.7 5.5 %copy.37 = bf16[192,8,8,256]{3,2,1,0:T(8,128)(2,1)S(1)} copy(bf16[192,8,8,256]{3,1,2,0:T(8,128)(2,1)} %bitcast.88) | data formatting | bytes 12582912
  122.2 0.8 fusion.18
  123.0 1.5 slice.57
  124.6 3.1 %fusion.19 = (bf16[8,256,16,32]{1,0,3,2:T(8,128)(2,1)}, bf16[8,256,16,32]{1,0,3,2:T(8,128)(2,1)}) fusion(f32[8,256,16]{1,0,2:T(8,128)S(1)} %get-tuple-element.53, bf16[8,256,3,16,32]{1,0,4,3,2:T(8,128)(2,1)S(1)} %bitcast.87, f32[8,256,16]{1,0,2:T(8,128)S(1)} %get-tuple-element.52), kind=kLoop, calls=%fused_computation.36 | loop fusion | flops 6291456 | bytes 8650752 | tf_op jit(solution)/shard_map/while/body/eval_jaxpr/convert_element_type | solution.py:54
  127.7 19.8 %fusion.82 = (f32[8,16,256]{2,1,0:T(8,128)S(1)}, f32[8,16,256,256]{2,3,1,0:T(8,128)}) fusion(f32[8,256,256]{1,2,0:T(8,128)} %compare_select_fusion, f32[16,256,256]{1,2,0:T(8,128)} %reshape.177, f32[16]{0:T(128)S(1)} %minimum_exponential_fusion, bf16[8,256,16,32]{1,0,3,2:T(8,128)(2,1)} %get-tuple-element.28, bf16[8,256,16,32]{1,0,3,2:T(8,128)(2,1)} %get-tuple-element.27), kind=kOutput, calls=%fused_computation.120 | convolution fusion | flops 578814208 | bytes 44171328 | tf_op jit(solution)/shard_map/while/body/eval_jaxpr/sub | solution.py:62
  147.5 15.0 %convert_bitcast_fusion = bf16[8,256,16,32]{1,3,2,0:T(8,128)(2,1)} fusion(f32[8,16,256,256]{2,3,1,0:T(8,128)} %get-tuple-element.46, f32[8,16,256]{2,1,0:T(8,128)S(1)} %get-tuple-element.44, bf16[8,256,1,16,32]{1,0,4,3,2:T(8,128)(2,1)} %slice.57), kind=kOutput, calls=%fused_computation.54 | convolution fusion | flops 554696704 | bytes 37879808 | tf_op jit(solution)/shard_map/while/body/eval_jaxpr/nhqk,nkhd->nqhd/dot_general | solution.py:64
  162.5 3.1 %copy.27 = bf16[8,256,16,32]{1,0,3,2:T(8,128)(2,1)S(1)} copy(bf16[8,256,16,32]{1,3,2,0:T(8,128)(2,1)} %convert_bitcast_fusion) | data formatting | bytes 4194304 | tf_op jit(solution)/shard_map/while/body/eval_jaxpr/convert_element_type | solution.py:66
  165.6 0.7 copy.38
  166.3 1.4 fusion.91
  167.7 0.0 copy-start.7
  167.7 0.0 copy-start.8
  167.7 0.8 multiply_reduce_fusion.1
  168.6 0.7 copy-done.3
  169.3 2.6 %add_convert_fusion.1 = bf16[2048,512]{1,0:T(8,128)(2,1)S(1)} fusion(f32[2048,512]{1,0:T(8,128)S(1)} %get-tuple-element.49, f32[512]{0:T(512)S(1)} %copy-done.7, f32[512]{0:T(512)S(1)} %copy-done.8, f32[2048]{0:T(1024)S(1)} %add_rsqrt_fusion.3, f32[2048]{0:T(1024)S(1)} %broadcast_multiply_fusion.1, f32[2048]{0:T(1024)S(1)} %bitcast.99, ...), kind=kLoop, calls=%fused_computation.41 | loop fusion | flops 8388608 | bytes 8417280 | tf_op jit(solution)/shard_map/while/body/eval_jaxpr/convert_element_type | solution.py:72
  171.9 0.2 copy.28
  172.1 39.6 %fusion.17.clone.4 = bf16[2048,2048]{1,0:T(8,128)(2,1)S(1)} fusion(bf16[2048,512]{1,0:T(8,128)(2,1)S(1)} %bitcast.93, bf16[512,2048]{1,0:T(8,128)(2,1)S(1)} %copy-done), kind=kOutput, calls=%fused_computation.8.clone.clone.clone.clone.1 | convolution fusion | flops 4567597056 | bytes 12582912 | tf_op jit(solution)/shard_map/dot_general | solution.py:77
  211.7 4.6 %fusion.92 = (f32[2048]{0:T(1024)S(1)}, f32[2048,512]{1,0:T(8,128)S(1)}) fusion(bf16[2048,512]{1,0:T(8,128)(2,1)S(1)} %copy-done.11, bf16[2048,2048]{1,0:T(8,128)(2,1)S(1)} %fusion.17.clone.4), kind=kOutput, calls=%fused_computation.122 | convolution fusion | flops 4296013824 | bytes 14688256 | tf_op jit(solution)/shard_map/dot_general | solution.py:79
  216.3 0.0 copy-start.10
  216.4 0.8 multiply_reduce_fusion
  217.2 2.6 %add_convert_fusion = bf16[2048,512]{1,0:T(8,128)(2,1)S(1)} fusion(f32[2048,512]{1,0:T(8,128)S(1)} %get-tuple-element.51, f32[512]{0:T(512)S(1)} %copy-done.9, f32[512]{0:T(512)S(1)} %copy-done.10, f32[2048]{0:T(1024)S(1)} %add_rsqrt_fusion.2, f32[2048]{0:T(1024)S(1)} %broadcast_multiply_fusion, f32[2048]{0:T(1024)S(1)} %copy-done.6, ...), kind=kLoop, calls=%fused_computation.39 | loop fusion | flops 8388608 | bytes 8417280 | tf_op jit(solution)/shard_map/convert_element_type | solution.py:82
  219.8 0.1 fusion.81
  220.0 0.1 collective-permute-start.2
  220.1 16.9 %collective-permute-done.2 = bf16[8,128,512]{2,1,0:T(8,128)(2,1)S(1)} collective-permute-done((bf16[8,128,512]{2,1,0:T(8,128)(2,1)S(1)}, bf16[8,128,512]{2,1,0:T(8,128)(2,1)S(1)}, u32[]{:S(2)}, u32[]{:S(2)}) %collective-permute-start.2) | collective-permute-done | bytes 1048608 | tf_op jit(solution)/shard_map/ppermute | solution.py:17
  237.0 0.6 collective-permute-start.3
  237.6 4.4 %collective-permute-done.3 = bf16[16,8,512]{2,1,0:T(8,128)(2,1)S(1)} collective-permute-done((bf16[16,8,512]{2,1,0:T(8,128)(2,1)S(1)}, bf16[16,8,512]{2,1,0:T(8,128)(2,1)S(1)}, u32[]{:S(2)}, u32[]{:S(2)}) %collective-permute-start.3) | collective-permute-done | bytes 131104 | tf_op jit(solution)/shard_map/ppermute | solution.py:17
  242.0 1.5 fusion.26
  (40 shorter events, 0.2 us)
Async XLA Ops:
  0.0 172.1 %copy-start = (bf16[512,2048]{1,0:T(8,128)(2,1)S(1)}, bf16[512,2048]{1,0:T(8,128)(2,1)}, u32[]{:S(2)}) copy-start(bf16[512,2048]{1,0:T(8,128)(2,1)} %param.16) | copy-start | bytes 6291460
  0.0 7.2 %copy-start.5 = (f32[16,31,31]{2,0,1:T(8,128)S(1)}, f32[16,31,31]{2,0,1:T(8,128)}, u32[]{:S(2)}) copy-start(f32[16,31,31]{2,0,1:T(8,128)} %param.19) | copy-start | bytes 184516
  1.1 24.6 %collective-permute-start = (bf16[16,8,512]{2,1,0:T(8,128)(2,1)S(1)}, bf16[16,8,512]{2,1,0:T(8,128)(2,1)S(1)}, u32[]{:S(2)}, u32[]{:S(2)}) collective-permute-start(bf16[16,8,512]{2,1,0:T(8,128)(2,1)S(1)} %slice.43), channel_id=1, source_target_pairs={{0,1},{1,0},{2,3},{3,2},{4,5},{5,4},{6,7},{7,6},{8,9},{9,8},{10,11... | collective-permute-start | bytes 393224 | tf_op jit(solution)/shard_map/ppermute | solution.py:17
  8.2 17.5 %copy-start.13 = (s32[1,8]{1,0:T(1,128)S(1)}, s32[1,8]{1,0:T(1,128)}, u32[]{:S(2)}) copy-start(s32[1,8]{1,0:T(1,128)} %param.13) | copy-start | bytes 100
  28.4 71.3 %collective-permute-start.1 = (bf16[8,128,512]{2,1,0:T(8,128)(2,1)}, bf16[8,128,512]{2,1,0:T(8,128)(2,1)}, u32[]{:S(2)}, u32[]{:S(2)}) collective-permute-start(bf16[8,128,512]{2,1,0:T(8,128)(2,1)} %get-tuple-element.32), channel_id=1, source_target_pairs={{0,30},{2,0},{4,2},{6,4},{8,6},{10,8},{12,10},{14,12},{16,14},{18,... | collective-permute-start | bytes 3145736 | tf_op jit(solution)/shard_map/ppermute | solution.py:17
  73.7 24.3 %copy-start.14 = (f32[16]{0:T(128)S(1)}, f32[16]{0:T(128)}, u32[]{:S(2)}) copy-start(f32[16]{0:T(128)} %param.18) | copy-start | bytes 196
  99.7 3.0 %copy-start.12 = (bf16[512,1536]{1,0:T(8,128)(2,1)S(1)}, bf16[512,1536]{1,0:T(8,128)(2,1)}, u32[]{:S(2)}) copy-start(bf16[512,1536]{1,0:T(8,128)(2,1)} %param.14) | copy-start | bytes 4718596
  101.4 1.3 copy-start.2
  162.5 3.8 %copy-start.4 = (bf16[512,512]{1,0:T(8,128)(2,1)S(1)}, bf16[512,512]{1,0:T(8,128)(2,1)}, u32[]{:S(2)}) copy-start(bf16[512,512]{1,0:T(8,128)(2,1)} %param.15) | copy-start | bytes 1572868
  167.7 1.6 copy-start.3
  167.7 1.6 copy-start.7
  167.7 1.6 copy-start.8
  172.1 39.6 %copy-start.11 = (bf16[2048,512]{1,0:T(8,128)(2,1)S(1)}, bf16[2048,512]{1,0:T(8,128)(2,1)}, u32[]{:S(2)}) copy-start(bf16[2048,512]{1,0:T(8,128)(2,1)} %param.17) | copy-start | bytes 6291460
  216.3 0.9 copy-start.6
  216.3 0.9 copy-start.9
  216.3 0.9 copy-start.10
  219.8 23.6 %copy-start.1 = (bf16[512,2048]{1,0:T(8,128)(2,1)S(1)}, bf16[512,2048]{1,0:T(8,128)(2,1)}, u32[]{:S(2)}) copy-start(bf16[512,2048]{1,0:T(8,128)(2,1)} %param.16) | copy-start | bytes 6291460
  220.0 17.0 %collective-permute-start.2 = (bf16[8,128,512]{2,1,0:T(8,128)(2,1)S(1)}, bf16[8,128,512]{2,1,0:T(8,128)(2,1)S(1)}, u32[]{:S(2)}, u32[]{:S(2)}) collective-permute-start(bf16[8,128,512]{2,1,0:T(8,128)(2,1)S(1)} %bitcast.97), channel_id=1, source_target_pairs={{0,2},{2,4},{4,6},{6,8},{8,10},{10,12},{12,14},{14,16},{16,18},{18... | collective-permute-start | bytes 3145736 | tf_op jit(solution)/shard_map/ppermute | solution.py:17
  237.0 5.0 %collective-permute-start.3 = (bf16[16,8,512]{2,1,0:T(8,128)(2,1)S(1)}, bf16[16,8,512]{2,1,0:T(8,128)(2,1)S(1)}, u32[]{:S(2)}, u32[]{:S(2)}) collective-permute-start(bf16[16,8,512]{2,1,0:T(8,128)(2,1)S(1)} %pad_maximum_fusion.3), channel_id=1, source_target_pairs={{0,1},{1,0},{2,3},{3,2},{4,5},{5,4},{6,7},{7,6},{8,9},{9,8},{10,11... | collective-permute-start | bytes 393224 | tf_op jit(solution)/shard_map/ppermute | solution.py:17
where the time goes:
time: 245 us; the launch traced here: 243 us
  matrix products  104 us (42%)
  local copies, waits for them, and re-layouts  92.1 us (38%)
  waiting for transfers between devices  21.4 us (9%)
  other arithmetic  18.3 us (7%)
  starting transfers between devices  7.38 us (3%)
    add x2, local copies, waits for them, and re-layouts, attend_windows(): scores * head_scale[None, :, None, None] + bias[None] + penalty[:, None]  64.9 us
    dot_general x1, matrix products, feed_forward(): jnp.dot(tokens, w_fc1, preferred_element_type=jnp.float32)  39.6 us
    ppermute x4, waiting for transfers between devices, shifted(): return lax.ppermute(x, axis, [(i, (i + by) % count) for i in range(count)])  21.4 us
    sub x1, matrix products, attend_windows(): raised = jnp.exp(scores - highest)  19.8 us
    dot_general x1, matrix products, full_bias(): jnp.einsum('xya,hauv->hxuyv', select, by_cols, precision=lax.Precision.HI...  17.4 us
    dot_general x1, matrix products, attend_windows(): jnp.einsum('nhqk,nkhd->nqhd', weights, values, preferred_element_type=jnp...  15 us
    convert_element_type x1, local copies, waits for them, and re-layouts, attend_windows(): jnp.dot(flat, w_qkv, preferred_element_type=jnp.float32)  8.67 us
    unnamed x34, local copies, waits for them, and re-layouts  8.35 us
  transfers between devices with their start and end apart: 4, of which 2 were waited for; matrix products, arithmetic and copies ran while one was open for 37% of the time, Pallas kernels for 0%

commit v1 on v0

v1 whole, which is shorter than its diff:
```python
import math

import jax
import jax.numpy as jnp
from jax import lax
from jax.experimental import pallas as pl
from jax.experimental.pallas import tpu as pltpu
from jax.sharding import PartitionSpec as P

DIM = 512
HEADS = 16
WIN = 16
HEAD_DIM = 32
SHIFT = 8
TOKENS = WIN * WIN
SPAN = 2 * WIN * WIN
LOG2E = math.log2(math.e)


def shifted(x, axis, by):
    count = lax.axis_size(axis)
    return lax.ppermute(x, axis, [(i, (i + by) % count) for i in range(count)])


def nt_dot(a, b):
    return lax.dot_general(a, b, (((1,), (1,)), ((), ())), preferred_element_type=jnp.float32)


def tn_dot(a, b):
    return lax.dot_general(a, b, (((0,), (0,)), ((), ())), preferred_element_type=jnp.float32)


def nn_dot(a, b):
    return lax.dot_general(a, b, (((1,), (0,)), ((), ())), preferred_element_type=jnp.float32)


def half_of(axis):
    key = lax.broadcasted_iota(jnp.int32, (TOKENS, TOKENS), 0)
    query = lax.broadcasted_iota(jnp.int32, (TOKENS, TOKENS), 1)
    if axis == 0:
        key, query = key // WIN, query // WIN
    else:
        key, query = key % WIN, query % WIN
    return (key < SHIFT) != (query < SHIFT)


def bias_kernel(edge_ref, low_ref, high_ref, bias_ref, rows_ref, pen_ref):
    low = low_ref[...]
    high = high_ref[...]
    place = lax.broadcasted_iota(jnp.int32, (HEADS, SPAN), 1) % WIN
    for y in range(WIN):
        s = WIN - 1 - y
        first = pltpu.roll(low, (SPAN - s) % SPAN, 1)
        second = pltpu.roll(high, WIN - s, 1)
        rows_ref[:, y, :] = jnp.where(place < WIN - s, first, second)
    by_row = half_of(0) & (edge_ref[0] == 1)
    by_col = half_of(1) & (edge_ref[1] == 1)
    row_pen = jnp.where(by_row, jnp.float32(-100.0 * LOG2E), jnp.float32(0.0))
    pen_ref[0] = row_pen
    pen_ref[1] = jnp.where(by_col, jnp.float32(-100.0 * LOG2E), row_pen)

    def one_head(h, carry):
        rows = rows_ref[h]
        for v in range(WIN):
            lanes = WIN * (WIN - 1 - v)
            moved = pltpu.roll(rows, (SPAN - lanes) % SPAN, 1)[:, :TOKENS]
            at = slice(v * WIN, (v + 1) * WIN)
            bias_ref[0, h, at, :] = moved + pen_ref[0, at, :]
            bias_ref[1, h, at, :] = moved + pen_ref[1, at, :]
        return carry

    lax.fori_loop(0, HEADS, one_head, 0)


def build_bias(edges, bias_table):
    table = jnp.pad(bias_table * jnp.float32(LOG2E), ((0, 0), (0, 1), (0, 1)))
    low = table[:, :, :WIN].reshape(HEADS, SPAN)
    high = table[:, :, WIN:].reshape(HEADS, SPAN)
    return pl.pallas_call(
        bias_kernel,
        out_shape=jax.ShapeDtypeStruct((2, HEADS, TOKENS, TOKENS), jnp.float32),
        in_specs=[
            pl.BlockSpec(memory_space=pltpu.SMEM),
            pl.BlockSpec(memory_space=pltpu.VMEM),
            pl.BlockSpec(memory_space=pltpu.VMEM),
        ],
        out_specs=pl.BlockSpec(memory_space=pltpu.VMEM),
        scratch_shapes=[
            pltpu.VMEM((HEADS, WIN, SPAN), jnp.float32),
            pltpu.VMEM((2, TOKENS, TOKENS), jnp.float32),
        ],
        compiler_params=pltpu.CompilerParams(vmem_limit_bytes=24 * 2**20),
        cost_estimate=pl.CostEstimate(
            flops=4 * 2**20, bytes_accessed=20 * 2**20, transcendentals=0
        ),
        name="bias",
    )(edges, low, high)


def layer_norm(values, gain, offset):
    centre = jnp.mean(values, axis=-1, keepdims=True)
    centred = values - centre
    spread = jnp.mean(centred * centred, axis=-1, keepdims=True)
    return centred * lax.rsqrt(spread + 1e-05) * gain + offset


def gelu(x):
    return 0.5 * x * (1.0 + lax.erf(x * jnp.float32(math.sqrt(0.5))))


def window_kernel(
    tissue_ref,
    scale_ref,
    x_ref,
    wqkv_ref,
    wproj_ref,
    wfc1_ref,
    wfc2_ref,
    bias_ref,
    norm_ref,
    out_ref,
    triple_ref,
    mixed_ref,
):
    w = pl.program_id(0)
    x = x_ref[...].reshape(TOKENS, DIM)
    triple = nt_dot(wqkv_ref[...], x).astype(jnp.bfloat16)
    for at in range(2):
        part = triple[at * DIM : (at + 1) * DIM].astype(jnp.float32)
        part = part.reshape(HEADS, HEAD_DIM, TOKENS)
        part = part * lax.rsqrt(jnp.sum(part * part, axis=1, keepdims=True) + 1e-06)
        triple_ref[at * DIM : (at + 1) * DIM, :] = part.reshape(DIM, TOKENS).astype(jnp.bfloat16)
    triple_ref[2 * DIM :, :] = triple[2 * DIM :]
    ones = jnp.ones((16, TOKENS), jnp.bfloat16)
    for h in range(HEADS):
        at = h * HEAD_DIM
        query = triple_ref[at : at + HEAD_DIM, :]
        key = triple_ref[DIM + at : DIM + at + HEAD_DIM, :]
        value = triple_ref[2 * DIM + at : 2 * DIM + at + HEAD_DIM, :]
        scores = tn_dot(key, query) * scale_ref[h] + bias_ref[0, h]
        highest = jnp.max(scores, axis=0, keepdims=True)
        raised = jnp.exp2(scores - highest).astype(jnp.bfloat16)
        both = nn_dot(jnp.concatenate([value, ones], axis=0), raised)
        mixed = both[:HEAD_DIM] * (1.0 / both[HEAD_DIM : HEAD_DIM + 1])
        mixed_ref[at : at + HEAD_DIM, :] = mixed.astype(jnp.bfloat16)
    keep = tissue_ref[0, w].astype(jnp.float32)
    projected = tn_dot(mixed_ref[...], wproj_ref[...])
    branch = layer_norm(projected, norm_ref[0:1, :], norm_ref[1:2, :])
    after = (x.astype(jnp.float32) + keep * branch).astype(jnp.bfloat16)
    hidden = gelu(nn_dot(after, wfc1_ref[...])).astype(jnp.bfloat16)
    grown = nn_dot(hidden, wfc2_ref[...])
    branch = layer_norm(grown, norm_ref[2:3, :], norm_ref[3:4, :])
    final = (after.astype(jnp.float32) + keep * branch).astype(jnp.bfloat16)
    out_ref[...] = final.reshape(WIN, WIN, DIM)


def run_windows(tissue, scale, rolled, weights, bias, norms):
    cols = rolled.shape[1]
    count = cols // WIN
    smem = pl.BlockSpec(memory_space=pltpu.SMEM)
    whole = pl.BlockSpec(memory_space=pltpu.VMEM)
    tile = pl.BlockSpec((WIN, WIN, DIM), lambda w: (0, w, 0))
    table = pl.BlockSpec(
        (1, HEADS, TOKENS, TOKENS), lambda w: (jnp.where(w == count - 1, 1, 0), 0, 0, 0)
    )
    return pl.pallas_call(
        window_kernel,
        grid=(count,),
        out_shape=jax.ShapeDtypeStruct(rolled.shape, jnp.bfloat16),
        in_specs=[smem, smem, tile] + [whole] * 4 + [table, whole],
        out_specs=tile,
        scratch_shapes=[
            pltpu.VMEM((3 * DIM, TOKENS), jnp.bfloat16),
            pltpu.VMEM((DIM, TOKENS), jnp.bfloat16),
        ],
        compiler_params=pltpu.CompilerParams(
            vmem_limit_bytes=48 * 2**20, dimension_semantics=("arbitrary",)
        ),
        cost_estimate=pl.CostEstimate(
            flops=count * 2 * 10**9, bytes_accessed=16 * 2**20, transcendentals=count * 2**20
        ),
        name="windows",
    )(tissue, scale, rolled, *weights, bias, norms)


def on_device(
    crop,
    tissue,
    w_qkv,
    w_proj,
    w_fc1,
    w_fc2,
    logit_scale,
    bias_table,
    norm1_gain,
    norm1_bias,
    norm2_gain,
    norm2_bias,
):
    tile_rows, tile_cols = (crop.shape[0], crop.shape[1])
    edges = jnp.stack(
        [
            (lax.axis_index("row") == lax.axis_size("row") - 1).astype(jnp.int32),
            (lax.axis_index("col") == lax.axis_size("col") - 1).astype(jnp.int32),
        ]
    )
    scale = jnp.exp(jnp.minimum(logit_scale, math.log(100.0))) * jnp.float32(LOG2E)
    weights = (w_qkv.T, w_proj, w_fc1, w_fc2)
    norms = jnp.stack([norm1_gain, norm1_bias, norm2_gain, norm2_bias])
    bias = build_bias(edges, bias_table)
    beside = shifted(crop[:, :SHIFT], "col", -1)
    widened = jnp.concatenate([crop[:, SHIFT:], beside], axis=1)
    below = shifted(widened[:SHIFT], "row", -1)
    rolled = jnp.concatenate([widened[SHIFT:], below], axis=0)
    finished = run_windows(tissue, scale, rolled, weights, bias, norms)
    above = shifted(finished[tile_rows - SHIFT :], "row", 1)
    lifted = jnp.concatenate([above, finished[: tile_rows - SHIFT]], axis=0)
    leftward = shifted(lifted[:, tile_cols - SHIFT :], "col", 1)
    return jnp.concatenate([leftward, lifted[:, : tile_cols - SHIFT]], axis=1)


def solution(mesh):
    in_specs = (P("row", "col", None), P("row", "col")) + (P(),) * 10
    return jax.shard_map(
        on_device,
        mesh=mesh,
        in_specs=in_specs,
        out_specs=P("row", "col", None),
        check_vma=False,
    )
```

time: 245 us -> 111 us (0.45)
  matrix products: 104 us -> 0 us
  local copies, waits for them, and re-layouts: 92.1 us -> 6.81 us
  Pallas kernels: 0 us -> 62.3 us
  other arithmetic: 18.3 us -> 5.58 us
  waiting for transfers between devices: 21.4 us -> 27.9 us
    dot_general x7 -> x0, matrix products: 84.3 us -> none  [the longest x1 39.6 us: feed_forward(): jnp.dot(tokens, w_fc1, preferred_element_type=jnp.float32)]
    add x6 -> x0, local copies, waits for them, and re-layouts: 65.2 us -> none  [the longest x2 64.9 us: attend_windows(): scores * head_scale[None, :, None, None] + bias[None] + penalty[:, None]]
    pallas_call x0 -> x2, Pallas kernels: none -> 62.3 us  [the longest x1 59.3 us: run_windows(): pl.pallas_call(window_kernel, grid=(count,), out_shape=jax.ShapeDtypeStru...]
    sub x1 -> x0, matrix products: 19.8 us -> none  [attend_windows(): raised = jnp.exp(scores - highest)]
    convert_element_type x2 -> x0, local copies, waits for them, and re-layouts: 11.7 us -> none  [the longest x1 8.67 us: attend_windows(): jnp.dot(flat, w_qkv, preferred_element_type=jnp.float32)]
    convert_element_type x3 -> x0, other arithmetic: 8.36 us -> none  [the longest x1 3.12 us: attend_windows(): unit_rows(triple[:, :, 0].astype(jnp.float32)).astype(jnp.bfloat16)]
    ppermute x4, waiting for transfers between devices: 21.4 us -> 27.9 us  [shifted(): return lax.ppermute(x, axis, [(i, (i + by) % count) for i in range(count)])]
    unnamed x34 -> x19, local copies, waits for them, and re-layouts: 8.35 us -> 4.97 us
  transfers between devices with their start and end apart: 4 -> 4, of which waited for: 2 -> 4; matrix products, arithmetic and copies ran while one was open for 37% -> 2% of each run, Pallas kernels for 0% -> 3%
where the time goes in v1:
time: 111 us
  Pallas kernels  62.3 us (56%)
  waiting for transfers between devices  27.9 us (25%)
  starting transfers between devices  8 us (7%)
  local copies, waits for them, and re-layouts  6.81 us (6%)
  other arithmetic  5.58 us (5%)
    pallas_call x1, Pallas kernels, run_windows(): pl.pallas_call(window_kernel, grid=(count,), out_shape=jax.ShapeDtypeStru...  59.3 us
    ppermute x4, waiting for transfers between devices, shifted(): return lax.ppermute(x, axis, [(i, (i + by) % count) for i in range(count)])  27.9 us
    ppermute x4, starting transfers between devices, shifted(): return lax.ppermute(x, axis, [(i, (i + by) % count) for i in range(count)])  8 us
    unnamed x19, local copies, waits for them, and re-layouts  4.97 us
    pallas_call x1, Pallas kernels, build_bias(): pl.pallas_call(bias_kernel, out_shape=jax.ShapeDtypeStruct((2, HEADS, TOK...  3.01 us
    concatenate x1, other arithmetic, on_device(): rolled = jnp.concatenate([widened[SHIFT:], below], axis=0)  2.78 us
  transfers between devices with their start and end apart: 4, of which 4 were waited for; matrix products, arithmetic and copies ran while one was open for 2% of the time, Pallas kernels for 3%

profile of v1, /device:TPU:0, one launch (start us, length us, event | category | flops | bytes accessed | tf_op | source)
XLA Modules:
  0.0 110.7 jit_solution(11387222227480636287)
XLA Ops:
  0.0 0.0 slice-start
  0.0 1.1 slice.31
  1.1 3.0 %collective-permute-start = (bf16[16,8,512]{2,1,0:T(8,128)(2,1)S(1)}, bf16[16,8,512]{2,1,0:T(8,128)(2,1)S(1)}, u32[]{:S(2)}, u32[]{:S(2)}) collective-permute-start(bf16[16,8,512]{2,1,0:T(8,128)(2,1)S(1)} %slice.31), channel_id=1, source_target_pairs={{0,1},{1,0},{2,3},{3,2},{4,5},{5,4},{6,7},{7,6},{8,9},{9,8},{10,11... | collective-permute-start | bytes 393224 | tf_op jit(solution)/shard_map/ppermute | solution.py:22
  4.1 0.0 copy-start.3
  4.1 3.5 %collective-permute-done = bf16[16,8,512]{2,1,0:T(8,128)(2,1)S(1)} collective-permute-done((bf16[16,8,512]{2,1,0:T(8,128)(2,1)S(1)}, bf16[16,8,512]{2,1,0:T(8,128)(2,1)S(1)}, u32[]{:S(2)}, u32[]{:S(2)}) %collective-permute-start) | collective-permute-done | bytes 131104 | tf_op jit(solution)/shard_map/ppermute | solution.py:22
  7.6 0.0 slice-done
  7.6 1.2 %fusion.1 = (bf16[8,128,512]{2,1,0:T(8,128)(2,1)S(1)}, bf16[8,128,512]{2,1,0:T(8,128)(2,1)}) fusion(bf16[16,120,512]{2,1,0:T(8,128)(2,1)S(1)} %slice-done, bf16[16,8,512]{2,1,0:T(8,128)(2,1)S(1)} %collective-permute-done), kind=kLoop, calls=%fused_computation.5 | loop fusion | flops 4194304 | bytes 4194304 | tf_op jit(solution)/shard_map/concatenate | solution.py:212
  8.8 3.4 %collective-permute-start.1 = (bf16[8,128,512]{2,1,0:T(8,128)(2,1)}, bf16[8,128,512]{2,1,0:T(8,128)(2,1)}, u32[]{:S(2)}, u32[]{:S(2)}) collective-permute-start(bf16[8,128,512]{2,1,0:T(8,128)(2,1)} %get-tuple-element.8), channel_id=1, source_target_pairs={{0,30},{2,0},{4,2},{6,4},{8,6},{10,8},{12,10},{14,12},{16,14},{18,... | collective-permute-start | bytes 3145736 | tf_op jit(solution)/shard_map/ppermute | solution.py:22
  12.1 0.0 copy-done.3
  12.2 0.1 pad_slice_fusion.2
  12.3 0.1 copy.18
  12.4 0.2 reshape.7.high_ref
  12.6 0.1 copy.17
  12.6 0.2 reshape.6.low_ref
  12.8 1.7 %copy.16 = bf16[512,1536]{0,1:T(8,128)(2,1)S(1)} copy(bf16[512,1536]{1,0:T(8,128)(2,1)} %param.14) | data formatting | bytes 3145728 | tf_op args[2]
  14.5 0.1 add_convert_fusion.edge_ref
  14.6 0.0 copy-start.4
  14.6 0.0 copy-start.5
  14.6 0.0 copy-start.6
  14.6 0.0 copy-start.7
  14.6 0.0 copy-start.8
  14.6 3.0 %bias.1.bias_ref = f32[2,16,256,256]{3,2,1,0:T(8,128)S(1)} custom-call(s32[2]{0:T(128)S(1)} %add_convert_fusion.edge_ref, f32[16,512]{1,0:T(8,128)S(1)} %reshape.6.low_ref, f32[16,512]{1,0:T(8,128)S(1)} %reshape.7.high_ref), custom_call_target="tpu_custom_call" | custom-call | flops 4194304 | bytes 20971520 | tf_op jit(solution)/shard_map/bias/pallas_call | solution.py:79
  17.6 0.0 copy-start
  17.7 3.2 %copy-done = f32[2,16,256,256]{3,2,1,0:T(8,128)} copy-done((f32[2,16,256,256]{3,2,1,0:T(8,128)}, f32[2,16,256,256]{3,2,1,0:T(8,128)S(1)}, u32[]{:S(2)}) %copy-start) | copy-done | bytes 8388632
  20.9 0.0 copy-done.4
  20.9 0.0 copy-done.5
  20.9 0.0 copy-done.6
  20.9 0.0 copy-done.7
  20.9 0.0 copy-done.8
  20.9 3.8 %collective-permute-done.1 = bf16[8,128,512]{2,1,0:T(8,128)(2,1)} collective-permute-done((bf16[8,128,512]{2,1,0:T(8,128)(2,1)}, bf16[8,128,512]{2,1,0:T(8,128)(2,1)}, u32[]{:S(2)}, u32[]{:S(2)}) %collective-permute-start.1) | collective-permute-done | bytes 1048608 | tf_op jit(solution)/shard_map/ppermute | solution.py:22
  24.8 0.0 copy-start.1
  24.8 0.0 copy-start.2
  24.8 2.8 %pad_maximum_fusion.1.x_ref = bf16[16,128,512]{2,1,0:T(8,128)(2,1)} fusion(bf16[8,128,512]{2,1,0:T(8,128)(2,1)} %collective-permute-done.1, bf16[8,128,512]{2,1,0:T(8,128)(2,1)S(1)} %get-tuple-element.7), kind=kLoop, calls=%fused_computation.4 | loop fusion | flops 1048576 | bytes 4194304 | tf_op jit(solution)/shard_map/concatenate | solution.py:214
  27.6 0.0 copy-done.1
  27.6 0.0 copy-done.2
  27.6 59.3 %windows.1 = bf16[16,128,512]{2,1,0:T(8,128)(2,1)S(1)} custom-call(s32[1,8]{1,0:T(1,128)S(1)} %copy-done.2, f32[16]{0:T(128)S(1)} %exponential_multiply_fusion.scale_ref, bf16[16,128,512]{2,1,0:T(8,128)(2,1)} %pad_maximum_fusion.1.x_ref, bf16[1536,512]{1,0:T(8,128)(2,1)S(1)} %bitcast.7, bf16[512,512]{1,0:T(8,128)(2,1)S(1)} %copy-done.1, ...), custom_call_target="tpu_custom_call" | custom-call | flops 16000000000 | bytes 16777216 | tf_op jit(solution)/shard_map/windows/pallas_call | solution.py:166
  86.9 0.2 fusion.2
  87.0 0.1 collective-permute-start.2
  87.1 17.1 %collective-permute-done.2 = bf16[8,128,512]{2,1,0:T(8,128)(2,1)S(1)} collective-permute-done((bf16[8,128,512]{2,1,0:T(8,128)(2,1)S(1)}, bf16[8,128,512]{2,1,0:T(8,128)(2,1)S(1)}, u32[]{:S(2)}, u32[]{:S(2)}) %collective-permute-start.2) | collective-permute-done | bytes 1048608 | tf_op jit(solution)/shard_map/ppermute | solution.py:22
  104.2 1.6 %collective-permute-start.3 = (bf16[16,8,512]{2,1,0:T(8,128)(2,1)S(1)}, bf16[16,8,512]{2,1,0:T(8,128)(2,1)S(1)}, u32[]{:S(2)}, u32[]{:S(2)}) collective-permute-start(bf16[16,8,512]{2,1,0:T(8,128)(2,1)S(1)} %pad_maximum_fusion.3), channel_id=1, source_target_pairs={{0,1},{1,0},{2,3},{3,2},{4,5},{5,4},{6,7},{7,6},{8,9},{9,8},{10,11... | collective-permute-start | bytes 393224 | tf_op jit(solution)/shard_map/ppermute | solution.py:22
  105.8 3.5 %collective-permute-done.3 = bf16[16,8,512]{2,1,0:T(8,128)(2,1)S(1)} collective-permute-done((bf16[16,8,512]{2,1,0:T(8,128)(2,1)S(1)}, bf16[16,8,512]{2,1,0:T(8,128)(2,1)S(1)}, u32[]{:S(2)}, u32[]{:S(2)}) %collective-permute-start.3) | collective-permute-done | bytes 131104 | tf_op jit(solution)/shard_map/ppermute | solution.py:22
  109.2 1.5 %fusion = bf16[16,128,512]{2,1,0:T(8,128)(2,1)} fusion(bf16[8,128,512]{2,1,0:T(8,128)(2,1)S(1)} %get-tuple-element.6, bf16[8,128,512]{2,1,0:T(8,128)(2,1)S(1)} %collective-permute-done.2, bf16[16,8,512]{2,1,0:T(8,128)(2,1)S(1)} %collective-permute-done.3), kind=kLoop, calls=%fused_computation.1 | loop fusion | flops 6291456 | bytes 4325376 | tf_op jit(solution)/shard_map/concatenate | solution.py:219
  (4 shorter events, 0.1 us)
Async XLA Ops:
  0.0 7.6 %slice-start = ((bf16[16,128,512]{2,1,0:T(8,128)(2,1)}), bf16[16,120,512]{2,1,0:T(8,128)(2,1)S(1)}, s32[]{:S(2)}) async-start(bf16[16,128,512]{2,1,0:T(8,128)(2,1)} %param.12), calls=%async_computation | async-start | bytes 3932160 | tf_op jit(solution)/shard_map/slice | solution.py:212
  1.1 6.5 %collective-permute-start = (bf16[16,8,512]{2,1,0:T(8,128)(2,1)S(1)}, bf16[16,8,512]{2,1,0:T(8,128)(2,1)S(1)}, u32[]{:S(2)}, u32[]{:S(2)}) collective-permute-start(bf16[16,8,512]{2,1,0:T(8,128)(2,1)S(1)} %slice.31), channel_id=1, source_target_pairs={{0,1},{1,0},{2,3},{3,2},{4,5},{5,4},{6,7},{7,6},{8,9},{9,8},{10,11... | collective-permute-start | bytes 393224 | tf_op jit(solution)/shard_map/ppermute | solution.py:22
  4.1 8.1 %copy-start.3 = (f32[16,31,31]{2,0,1:T(8,128)S(1)}, f32[16,31,31]{2,0,1:T(8,128)}, u32[]{:S(2)}) copy-start(f32[16,31,31]{2,0,1:T(8,128)} %param.19) | copy-start | bytes 184516
  8.8 16.0 %collective-permute-start.1 = (bf16[8,128,512]{2,1,0:T(8,128)(2,1)}, bf16[8,128,512]{2,1,0:T(8,128)(2,1)}, u32[]{:S(2)}, u32[]{:S(2)}) collective-permute-start(bf16[8,128,512]{2,1,0:T(8,128)(2,1)} %get-tuple-element.8), channel_id=1, source_target_pairs={{0,30},{2,0},{4,2},{6,4},{8,6},{10,8},{12,10},{14,12},{16,14},{18,... | collective-permute-start | bytes 3145736 | tf_op jit(solution)/shard_map/ppermute | solution.py:22
  14.6 6.3 %copy-start.4 = (f32[512]{0:T(512)S(1)}, f32[512]{0:T(512)}, u32[]{:S(2)}) copy-start(f32[512]{0:T(512)} %param.23) | copy-start | bytes 6148
  14.6 6.3 %copy-start.5 = (f32[512]{0:T(512)S(1)}, f32[512]{0:T(512)}, u32[]{:S(2)}) copy-start(f32[512]{0:T(512)} %param.22) | copy-start | bytes 6148
  14.6 6.3 %copy-start.6 = (f32[512]{0:T(512)S(1)}, f32[512]{0:T(512)}, u32[]{:S(2)}) copy-start(f32[512]{0:T(512)} %param.21) | copy-start | bytes 6148
  14.6 6.3 %copy-start.7 = (f32[512]{0:T(512)S(1)}, f32[512]{0:T(512)}, u32[]{:S(2)}) copy-start(f32[512]{0:T(512)} %param.20) | copy-start | bytes 6148
  14.6 6.3 %copy-start.8 = (f32[16]{0:T(128)S(1)}, f32[16]{0:T(128)}, u32[]{:S(2)}) copy-start(f32[16]{0:T(128)} %param.18) | copy-start | bytes 196
  17.6 3.2 %copy-start = (f32[2,16,256,256]{3,2,1,0:T(8,128)}, f32[2,16,256,256]{3,2,1,0:T(8,128)S(1)}, u32[]{:S(2)}) copy-start(f32[2,16,256,256]{3,2,1,0:T(8,128)S(1)} %bias.1.bias_ref) | copy-start | bytes 25165828
  24.8 2.8 %copy-start.1 = (bf16[512,512]{1,0:T(8,128)(2,1)S(1)}, bf16[512,512]{1,0:T(8,128)(2,1)}, u32[]{:S(2)}) copy-start(bf16[512,512]{1,0:T(8,128)(2,1)} %wproj_ref.1) | copy-start | bytes 1572868
  24.8 2.8 %copy-start.2 = (s32[1,8]{1,0:T(1,128)S(1)}, s32[1,8]{1,0:T(1,128)}, u32[]{:S(2)}) copy-start(s32[1,8]{1,0:T(1,128)} %tissue_ref.1) | copy-start | bytes 100
  87.0 17.1 %collective-permute-start.2 = (bf16[8,128,512]{2,1,0:T(8,128)(2,1)S(1)}, bf16[8,128,512]{2,1,0:T(8,128)(2,1)S(1)}, u32[]{:S(2)}, u32[]{:S(2)}) collective-permute-start(bf16[8,128,512]{2,1,0:T(8,128)(2,1)S(1)} %get-tuple-element.5), channel_id=1, source_target_pairs={{0,2},{2,4},{4,6},{6,8},{8,10},{10,12},{12,14},{14,16},{16,18},{18... | collective-permute-start | bytes 3145736 | tf_op jit(solution)/shard_map/ppermute | solution.py:22
  104.2 5.0 %collective-permute-start.3 = (bf16[16,8,512]{2,1,0:T(8,128)(2,1)S(1)}, bf16[16,8,512]{2,1,0:T(8,128)(2,1)S(1)}, u32[]{:S(2)}, u32[]{:S(2)}) collective-permute-start(bf16[16,8,512]{2,1,0:T(8,128)(2,1)S(1)} %pad_maximum_fusion.3), channel_id=1, source_target_pairs={{0,1},{1,0},{2,3},{3,2},{4,5},{5,4},{6,7},{7,6},{8,9},{9,8},{10,11... | collective-permute-start | bytes 393224 | tf_op jit(solution)/shard_map/ppermute | solution.py:22

commit v2 on v1

--- a/solution.py
+++ b/solution.py
@@ -1,3 +1,4 @@
+import functools
 import math
 
 import jax
@@ -22,6 +23,16 @@
     return lax.ppermute(x, axis, [(i, (i + by) % count) for i in range(count)])
 
 
+def shifted_both(x, by):
+    rows, cols = (lax.axis_size("row"), lax.axis_size("col"))
+    pairs = [
+        (r * cols + c, (r + by) % rows * cols + (c + by) % cols)
+        for r in range(rows)
+        for c in range(cols)
+    ]
+    return lax.ppermute(x, ("row", "col"), pairs)
+
+
 def nt_dot(a, b):
     return lax.dot_general(a, b, (((1,), (1,)), ((), ())), preferred_element_type=jnp.float32)
 
@@ -44,7 +55,7 @@
     return (key < SHIFT) != (query < SHIFT)
 
 
-def bias_kernel(edge_ref, low_ref, high_ref, bias_ref, rows_ref, pen_ref):
+def bias_kernel(edge_ref, low_ref, high_ref, inner_ref, last_ref, rows_ref, pen_ref):
     low = low_ref[...]
     high = high_ref[...]
     place = lax.broadcasted_iota(jnp.int32, (HEADS, SPAN), 1) % WIN
@@ -65,8 +76,8 @@
             lanes = WIN * (WIN - 1 - v)
             moved = pltpu.roll(rows, (SPAN - lanes) % SPAN, 1)[:, :TOKENS]
             at = slice(v * WIN, (v + 1) * WIN)
-            bias_ref[0, h, at, :] = moved + pen_ref[0, at, :]
-            bias_ref[1, h, at, :] = moved + pen_ref[1, at, :]
+            inner_ref[h, at, :] = moved + pen_ref[0, at, :]
+            last_ref[h, at, :] = moved + pen_ref[1, at, :]
         return carry
 
     lax.fori_loop(0, HEADS, one_head, 0)
@@ -78,13 +89,13 @@
     high = table[:, :, WIN:].reshape(HEADS, SPAN)
     return pl.pallas_call(
         bias_kernel,
-        out_shape=jax.ShapeDtypeStruct((2, HEADS, TOKENS, TOKENS), jnp.float32),
+        out_shape=[jax.ShapeDtypeStruct((HEADS, TOKENS, TOKENS), jnp.float32)] * 2,
         in_specs=[
             pl.BlockSpec(memory_space=pltpu.SMEM),
             pl.BlockSpec(memory_space=pltpu.VMEM),
             pl.BlockSpec(memory_space=pltpu.VMEM),
         ],
-        out_specs=pl.BlockSpec(memory_space=pltpu.VMEM),
+        out_specs=[pl.BlockSpec(memory_space=pltpu.VMEM)] * 2,
         scratch_shapes=[
             pltpu.VMEM((HEADS, WIN, SPAN), jnp.float32),
             pltpu.VMEM((2, TOKENS, TOKENS), jnp.float32),
@@ -109,21 +120,27 @@
 
 
 def window_kernel(
+    first,
     tissue_ref,
     scale_ref,
-    x_ref,
+    top_ref,
+    bottom_ref,
     wqkv_ref,
     wproj_ref,
     wfc1_ref,
     wfc2_ref,
+    norm_ref,
     bias_ref,
-    norm_ref,
-    out_ref,
+    top_out_ref,
+    bottom_out_ref,
     triple_ref,
     mixed_ref,
 ):
     w = pl.program_id(0)
-    x = x_ref[...].reshape(TOKENS, DIM)
+    half = SHIFT * WIN
+    x = jnp.concatenate(
+        [top_ref[...].reshape(half, DIM), bottom_ref[...].reshape(half, DIM)], axis=0
+    )
     triple = nt_dot(wqkv_ref[...], x).astype(jnp.bfloat16)
     for at in range(2):
         part = triple[at * DIM : (at + 1) * DIM].astype(jnp.float32)
@@ -137,13 +154,13 @@
         query = triple_ref[at : at + HEAD_DIM, :]
         key = triple_ref[DIM + at : DIM + at + HEAD_DIM, :]
         value = triple_ref[2 * DIM + at : 2 * DIM + at + HEAD_DIM, :]
-        scores = tn_dot(key, query) * scale_ref[h] + bias_ref[0, h]
+        scores = tn_dot(key, query) * scale_ref[h] + bias_ref[h]
         highest = jnp.max(scores, axis=0, keepdims=True)
         raised = jnp.exp2(scores - highest).astype(jnp.bfloat16)
         both = nn_dot(jnp.concatenate([value, ones], axis=0), raised)
         mixed = both[:HEAD_DIM] * (1.0 / both[HEAD_DIM : HEAD_DIM + 1])
         mixed_ref[at : at + HEAD_DIM, :] = mixed.astype(jnp.bfloat16)
-    keep = tissue_ref[0, w].astype(jnp.float32)
+    keep = tissue_ref[0, first + w].astype(jnp.float32)
     projected = tn_dot(mixed_ref[...], wproj_ref[...])
     branch = layer_norm(projected, norm_ref[0:1, :], norm_ref[1:2, :])
     after = (x.astype(jnp.float32) + keep * branch).astype(jnp.bfloat16)
@@ -151,36 +168,34 @@
     grown = nn_dot(hidden, wfc2_ref[...])
     branch = layer_norm(grown, norm_ref[2:3, :], norm_ref[3:4, :])
     final = (after.astype(jnp.float32) + keep * branch).astype(jnp.bfloat16)
-    out_ref[...] = final.reshape(WIN, WIN, DIM)
-
-
-def run_windows(tissue, scale, rolled, weights, bias, norms):
-    cols = rolled.shape[1]
-    count = cols // WIN
+    top_out_ref[...] = final[:half].reshape(SHIFT, WIN, DIM)
+    bottom_out_ref[...] = final[half:].reshape(SHIFT, WIN, DIM)
+
+
+def run_windows(first, tissue, scale, top, bottom, weights, norms, bias):
+    count = top.shape[1] // WIN
     smem = pl.BlockSpec(memory_space=pltpu.SMEM)
     whole = pl.BlockSpec(memory_space=pltpu.VMEM)
-    tile = pl.BlockSpec((WIN, WIN, DIM), lambda w: (0, w, 0))
-    table = pl.BlockSpec(
-        (1, HEADS, TOKENS, TOKENS), lambda w: (jnp.where(w == count - 1, 1, 0), 0, 0, 0)
-    )
+    tile = pl.BlockSpec((SHIFT, WIN, DIM), lambda w: (0, w, 0))
+    half = jax.ShapeDtypeStruct(top.shape, jnp.bfloat16)
     return pl.pallas_call(
-        window_kernel,
+        functools.partial(window_kernel, first),
         grid=(count,),
-        out_shape=jax.ShapeDtypeStruct(rolled.shape, jnp.bfloat16),
-        in_specs=[smem, smem, tile] + [whole] * 4 + [table, whole],
-        out_specs=tile,
+        out_shape=[half, half],
+        in_specs=[smem, smem, tile, tile] + [whole] * 6,
+        out_specs=[tile, tile],
         scratch_shapes=[
             pltpu.VMEM((3 * DIM, TOKENS), jnp.bfloat16),
             pltpu.VMEM((DIM, TOKENS), jnp.bfloat16),
         ],
         compiler_params=pltpu.CompilerParams(
-            vmem_limit_bytes=48 * 2**20, dimension_semantics=("arbitrary",)
+            vmem_limit_bytes=32 * 2**20, dimension_semantics=("arbitrary",)
         ),
         cost_estimate=pl.CostEstimate(
-            flops=count * 2 * 10**9, bytes_accessed=16 * 2**20, transcendentals=count * 2**20
+            flops=count * 7 * 10**9, bytes_accessed=4 * 2**20, transcendentals=count * 2**20
         ),
         name="windows",
-    )(tissue, scale, rolled, *weights, bias, norms)
+    )(tissue, scale, top, bottom, *weights, norms, bias)
 
 
 def on_device(
@@ -197,7 +212,7 @@
     norm2_gain,
     norm2_bias,
 ):
-    tile_rows, tile_cols = (crop.shape[0], crop.shape[1])
+    tile_cols = crop.shape[1]
     edges = jnp.stack(
         [
             (lax.axis_index("row") == lax.axis_size("row") - 1).astype(jnp.int32),
@@ -207,16 +222,35 @@
     scale = jnp.exp(jnp.minimum(logit_scale, math.log(100.0))) * jnp.float32(LOG2E)
     weights = (w_qkv.T, w_proj, w_fc1, w_fc2)
     norms = jnp.stack([norm1_gain, norm1_bias, norm2_gain, norm2_bias])
-    bias = build_bias(edges, bias_table)
-    beside = shifted(crop[:, :SHIFT], "col", -1)
-    widened = jnp.concatenate([crop[:, SHIFT:], beside], axis=1)
-    below = shifted(widened[:SHIFT], "row", -1)
-    rolled = jnp.concatenate([widened[SHIFT:], below], axis=0)
-    finished = run_windows(tissue, scale, rolled, weights, bias, norms)
-    above = shifted(finished[tile_rows - SHIFT :], "row", 1)
-    lifted = jnp.concatenate([above, finished[: tile_rows - SHIFT]], axis=0)
-    leftward = shifted(lifted[:, tile_cols - SHIFT :], "col", 1)
-    return jnp.concatenate([leftward, lifted[:, : tile_cols - SHIFT]], axis=1)
+    inner_bias, last_bias = build_bias(edges, bias_table)
+    windows = tile_cols // WIN
+    bounds = [windows, windows - 1, windows * 5 // 8, windows // 4, 0]
+    parts = [(lo, hi) for hi, lo in zip(bounds, bounds[1:]) if hi > lo]
+    side = shifted(crop[SHIFT:, :SHIFT], "col", -1)
+    corner = shifted_both(crop[:SHIFT, :SHIFT], -1)
+    tops, bottoms = ([], [])
+    for lo, hi in parts:
+        start, stop = (lo * WIN + SHIFT, hi * WIN + SHIFT)
+        top = crop[SHIFT:, start : min(stop, tile_cols)]
+        bottom = shifted(crop[:SHIFT, start : min(stop, tile_cols)], "row", -1)
+        if stop > tile_cols:
+            top = jnp.concatenate([top, side], axis=1)
+            bottom = jnp.concatenate([bottom, corner], axis=1)
+        tops.append(top)
+        bottoms.append(bottom)
+    own, above = ([], [])
+    for (lo, hi), top, bottom in zip(parts, tops, bottoms):
+        bias = last_bias if hi == windows else inner_bias
+        top, bottom = run_windows(lo, tissue, scale, top, bottom, weights, norms, bias)
+        if hi == windows:
+            from_left = shifted(top[:, -SHIFT:], "col", 1)
+            from_corner = shifted_both(bottom[:, -SHIFT:], 1)
+            top, bottom = (top[:, :-SHIFT], bottom[:, :-SHIFT])
+        own.insert(0, top)
+        above.insert(0, shifted(bottom, "row", 1))
+    upper = jnp.concatenate([from_corner] + above, axis=1)
+    lower = jnp.concatenate([from_left] + own, axis=1)
+    return jnp.concatenate([upper, lower], axis=0)
 
 
 def solution(mesh):

time: 111 us -> 105 us (0.946)
  waiting for transfers between devices: 27.9 us -> 12.7 us
  starting transfers between devices: 8 us -> 15.6 us
  local copies, waits for them, and re-layouts: 6.81 us -> 9.77 us
  Pallas kernels: 62.3 us -> 61.1 us
    ppermute x4 -> x10, waiting for transfers between devices: 27.9 us -> 12.5 us  [shifted(): return lax.ppermute(x, axis, [(i, (i + by) % count) for i in range(count)])]
    ppermute x4 -> x10, starting transfers between devices: 8 us -> 12.3 us  [shifted(): return lax.ppermute(x, axis, [(i, (i + by) % count) for i in range(count)])]
    ppermute x0 -> x2, starting transfers between devices: none -> 3.23 us  [shifted_both(): return lax.ppermute(x, ('row', 'col'), pairs)]
    slice x4 -> x5, local copies, waits for them, and re-layouts: 1.24 us -> 4.08 us  [the longest x3 4.06 us: on_device(): bottom = shifted(crop[:SHIFT, start:min(stop, tile_cols)], 'row', -1)]
    concatenate x3, other arithmetic: 5.45 us -> 3.23 us  [the longest x1 1.5 us: on_device(): return jnp.concatenate([upper, lower], axis=0)]
    pallas_call x2 -> x5, Pallas kernels: 62.3 us -> 61.1 us  [the longest x4 58.1 us: run_windows(): pl.pallas_call(functools.partial(window_kernel, first), grid=(count,), ou...]
    unnamed x19 -> x25, local copies, waits for them, and re-layouts: 4.97 us -> 5.07 us
  transfers between devices with their start and end apart: 4 -> 12, of which waited for: 4 -> 3; matrix products, arithmetic and copies ran while one was open for 2% -> 8% of each run, Pallas kernels for 3% -> 59%
where the time goes in v2:
time: 105 us; the launch traced here: 104 us
  Pallas kernels  61.1 us (58%)
  starting transfers between devices  15.6 us (15%)
  waiting for transfers between devices  12.7 us (12%)
  local copies, waits for them, and re-layouts  9.77 us (9%)
  other arithmetic  4.71 us (4%)
    pallas_call x4, Pallas kernels, run_windows(): pl.pallas_call(functools.partial(window_kernel, first), grid=(count,), ou...  58.1 us
    ppermute x10, waiting for transfers between devices, shifted(): return lax.ppermute(x, axis, [(i, (i + by) % count) for i in range(count)])  12.5 us
    ppermute x10, starting transfers between devices, shifted(): return lax.ppermute(x, axis, [(i, (i + by) % count) for i in range(count)])  12.3 us
    unnamed x25, local copies, waits for them, and re-layouts  5.07 us
    slice x3, local copies, waits for them, and re-layouts, on_device(): bottom = shifted(crop[:SHIFT, start:min(stop, tile_cols)], 'row', -1)  4.06 us
    ppermute x2, starting transfers between devices, shifted_both(): return lax.ppermute(x, ('row', 'col'), pairs)  3.23 us
    pallas_call x1, Pallas kernels, build_bias(): pl.pallas_call(bias_kernel, out_shape=[jax.ShapeDtypeStruct((HEADS, TOKEN...  3.03 us
  transfers between devices with their start and end apart: 12, of which 3 were waited for; matrix products, arithmetic and copies ran while one was open for 8% of the time, Pallas kernels for 59%

profile of v2, /device:TPU:0, one launch (start us, length us, event | category | flops | bytes accessed | tf_op | source)
XLA Modules:
  0.0 104.2 jit_solution(17878318395930532654)
XLA Ops:
  0.0 1.6 %fusion.2 = (bf16[8,8,512]{2,1,0:T(8,128)(2,1)}, bf16[8,8,512]{2,1,0:T(8,128)(2,1)}, bf16[8,8,512]{2,1,0:T(8,128)(2,1)}, bf16[8,8,512]{2,1,0:T(8,128)(2,1)S(1)}) fusion(bf16[16,128,512]{2,1,0:T(8,128)(2,1)} %param.12), kind=kLoop, calls=%fused_computation.21 | loop fusion | bytes 524288 | tf_op jit(solution)/shard_map/slice | solution.py:235
  1.6 5.4 %collective-permute-start.1 = (bf16[8,8,512]{2,1,0:T(8,128)(2,1)}, bf16[8,8,512]{2,1,0:T(8,128)(2,1)}, u32[]{:S(2)}, u32[]{:S(2)}) collective-permute-start(bf16[8,8,512]{2,1,0:T(8,128)(2,1)} %get-tuple-element.31), channel_id=1, source_target_pairs={{0,30},{2,0},{4,2},{6,4},{8,6},{10,8},{12,10},{14,12},{16,14},{18,... | collective-permute-start | bytes 196616 | tf_op jit(solution)/shard_map/ppermute | solution.py:23
  7.1 1.6 %collective-permute-start.2 = (bf16[8,8,512]{2,1,0:T(8,128)(2,1)}, bf16[8,8,512]{2,1,0:T(8,128)(2,1)}, u32[]{:S(2)}, u32[]{:S(2)}) collective-permute-start(bf16[8,8,512]{2,1,0:T(8,128)(2,1)} %get-tuple-element.32), channel_id=1, source_target_pairs={{0,31},{1,30},{2,1},{3,0},{4,3},{5,2},{6,5},{7,4},{8,7},{9,6},{10,... | collective-permute-start | bytes 196616 | tf_op jit(solution)/shard_map/ppermute | solution.py:33
  8.7 0.5 collective-permute-start
  9.2 1.3 %fusion = (bf16[8,32,512]{2,1,0:T(8,128)(2,1)S(1)}, bf16[8,32,512]{2,1,0:T(8,128)(2,1)S(1)}, bf16[8,32,512]{2,1,0:T(8,128)(2,1)S(1)}, bf16[8,32,512]{2,1,0:T(8,128)(2,1)S(1)}) fusion(bf16[16,128,512]{2,1,0:T(8,128)(2,1)} %param.12), kind=kLoop, calls=%fused_computation.19 | loop fusion | bytes 2097152 | tf_op jit(solution)/shard_map/slice | solution.py:235
  10.5 0.1 collective-permute-start.4
  10.6 0.1 pad_slice_fusion
  10.7 0.1 copy.17
  10.8 0.2 reshape.6.low_ref
  11.0 0.0 copy-start.7
  11.0 0.1 copy.18
  11.1 0.0 copy-start.3
  11.1 0.0 copy-start.4
  11.1 0.2 reshape.7.high_ref
  11.3 1.7 %copy.16 = bf16[512,1536]{0,1:T(8,128)(2,1)S(1)} copy(bf16[512,1536]{1,0:T(8,128)(2,1)} %param.14) | data formatting | bytes 3145728 | tf_op args[2]
  13.0 0.7 exponential_multiply_fusion.scale_ref
  13.7 0.1 add_convert_fusion.edge_ref
  13.7 3.0 %bias.1 = (f32[16,256,256]{2,1,0:T(8,128)S(1)}, f32[16,256,256]{2,1,0:T(8,128)S(1)}) custom-call(s32[2]{0:T(128)S(1)} %add_convert_fusion.edge_ref, f32[16,512]{1,0:T(8,128)S(1)} %reshape.6.low_ref, f32[16,512]{1,0:T(8,128)S(1)} %reshape.7.high_ref), custom_call_target="tpu_custom_call" | custom-call | flops 4194304 | bytes 20971520 | tf_op jit(solution)/shard_map/bias/pallas_call | solution.py:90
  16.8 0.7 pad_maximum_fusion.3.norm_ref
  17.5 0.0 collective-permute-done.1
  17.5 0.0 collective-permute-done.2
  17.5 0.9 pad_maximum_fusion.2.bottom_ref
  18.4 0.0 collective-permute-done
  18.4 0.8 pad_maximum_fusion.1.top_ref
  19.3 0.0 copy-start
  19.3 1.6 %copy-done = bf16[512,2048]{1,0:T(8,128)(2,1)S(1)} copy-done((bf16[512,2048]{1,0:T(8,128)(2,1)S(1)}, bf16[512,2048]{1,0:T(8,128)(2,1)}, u32[]{:S(2)}) %copy-start) | copy-done | bytes 2097176
  20.9 1.6 %copy-done.2 = bf16[2048,512]{1,0:T(8,128)(2,1)S(1)} copy-done((bf16[2048,512]{1,0:T(8,128)(2,1)S(1)}, bf16[2048,512]{1,0:T(8,128)(2,1)}, u32[]{:S(2)}) %copy-start.2) | copy-done | bytes 2097176
  22.5 7.5 %windows.4 = (bf16[8,16,512]{2,1,0:T(8,128)(2,1)S(1)}, bf16[8,16,512]{2,1,0:T(8,128)(2,1)S(1)}) custom-call(s32[1,8]{1,0:T(1,128)S(1)} %copy-done.4, f32[16]{0:T(128)S(1)} %exponential_multiply_fusion.scale_ref, bf16[8,16,512]{2,1,0:T(8,128)(2,1)S(1)} %pad_maximum_fusion.1.top_ref, bf16[8,16,512]{2,1,0:T(8,128)(2,1)S(1)} %pad_maximum_fusion.2.bottom_ref, ...), custom_call_target="tpu_custom_call" | custom-call | flops 7000000000 | bytes 4194304 | tf_op jit(solution)/shard_map/windows/pallas_call | solution.py:181
  30.0 0.0 copy-start.1
  30.0 1.6 %collective-permute-start.3 = (bf16[8,8,512]{2,1,0:T(8,128)(2,1)S(1)}, bf16[8,8,512]{2,1,0:T(8,128)(2,1)S(1)}, u32[]{:S(2)}, u32[]{:S(2)}) collective-permute-start(bf16[8,8,512]{2,1,0:T(8,128)(2,1)S(1)} %get-tuple-element.38), channel_id=1, source_target_pairs={{0,3},{1,2},{2,5},{3,4},{4,7},{5,6},{6,9},{7,8},{8,11},{9,10},{10,... | collective-permute-start | bytes 196616 | tf_op jit(solution)/shard_map/ppermute | solution.py:33
  31.6 1.2 %fusion.1 = (bf16[8,48,512]{2,1,0:T(8,128)(2,1)S(1)}, bf16[8,48,512]{2,1,0:T(8,128)(2,1)S(1)}) fusion(bf16[16,128,512]{2,1,0:T(8,128)(2,1)} %param.12), kind=kLoop, calls=%fused_computation.20 | loop fusion | bytes 1572864 | tf_op jit(solution)/shard_map/slice | solution.py:235
  32.8 3.8 %collective-permute-start.6 = (bf16[8,48,512]{2,1,0:T(8,128)(2,1)S(1)}, bf16[8,48,512]{2,1,0:T(8,128)(2,1)S(1)}, u32[]{:S(2)}, u32[]{:S(2)}) collective-permute-start(bf16[8,48,512]{2,1,0:T(8,128)(2,1)S(1)} %get-tuple-element.29), channel_id=1, source_target_pairs={{0,30},{2,0},{4,2},{6,4},{8,6},{10,8},{12,10},{14,12},{16,14},{18,... | collective-permute-start | bytes 1179656 | tf_op jit(solution)/shard_map/ppermute | solution.py:23
  36.6 0.1 collective-permute-start.8
  36.7 0.4 collective-permute-start.10
  37.2 0.2 collective-permute-done.3
  37.4 1.5 %collective-permute-start.11 = (bf16[8,8,512]{2,1,0:T(8,128)(2,1)S(1)}, bf16[8,8,512]{2,1,0:T(8,128)(2,1)S(1)}, u32[]{:S(2)}, u32[]{:S(2)}) collective-permute-start(bf16[8,8,512]{2,1,0:T(8,128)(2,1)S(1)} %slice.62), channel_id=1, source_target_pairs={{0,1},{1,0},{2,3},{3,2},{4,5},{5,4},{6,7},{7,6},{8,9},{9,8},{10,11... | collective-permute-start | bytes 196616 | tf_op jit(solution)/shard_map/ppermute | solution.py:23
  38.9 2.7 %collective-permute-done.11 = bf16[8,8,512]{2,1,0:T(8,128)(2,1)S(1)} collective-permute-done((bf16[8,8,512]{2,1,0:T(8,128)(2,1)S(1)}, bf16[8,8,512]{2,1,0:T(8,128)(2,1)S(1)}, u32[]{:S(2)}, u32[]{:S(2)}) %collective-permute-start.11) | collective-permute-done | bytes 65568 | tf_op jit(solution)/shard_map/ppermute | solution.py:23
  41.7 14.5 %windows.5 = (bf16[8,32,512]{2,1,0:T(8,128)(2,1)S(1)}, bf16[8,32,512]{2,1,0:T(8,128)(2,1)S(1)}) custom-call(s32[1,8]{1,0:T(1,128)S(1)} %copy-done.4, f32[16]{0:T(128)S(1)} %exponential_multiply_fusion.scale_ref, bf16[8,32,512]{2,1,0:T(8,128)(2,1)S(1)} %get-tuple-element.27.top_ref, bf16[8,32,512]{2,1,0:T(8,128)(2,1)S(1)} %collective-permute-done.4.bottom_ref, ...), custom_call_target="tpu_custom_call" | custom-call | flops 14000000000 | bytes 4194304 | tf_op jit(solution)/shard_map/windows/pallas_call | solution.py:181
  56.2 0.1 collective-permute-start.5
  56.3 0.0 collective-permute-done.8.bottom_ref
  56.3 14.5 %windows.7 = (bf16[8,32,512]{2,1,0:T(8,128)(2,1)S(1)}, bf16[8,32,512]{2,1,0:T(8,128)(2,1)S(1)}) custom-call(s32[1,8]{1,0:T(1,128)S(1)} %copy-done.4, f32[16]{0:T(128)S(1)} %exponential_multiply_fusion.scale_ref, bf16[8,32,512]{2,1,0:T(8,128)(2,1)S(1)} %get-tuple-element.28.top_ref, bf16[8,32,512]{2,1,0:T(8,128)(2,1)S(1)} %collective-permute-done.8.bottom_ref, ...), custom_call_target="tpu_custom_call" | custom-call | flops 14000000000 | bytes 4194304 | tf_op jit(solution)/shard_map/windows/pallas_call | solution.py:181
  70.8 0.3 collective-permute-start.9
  71.2 0.0 collective-permute-done.6.bottom_ref
  71.2 21.5 %windows.6 = (bf16[8,48,512]{2,1,0:T(8,128)(2,1)S(1)}, bf16[8,48,512]{2,1,0:T(8,128)(2,1)S(1)}) custom-call(s32[1,8]{1,0:T(1,128)S(1)} %copy-done.4, f32[16]{0:T(128)S(1)} %exponential_multiply_fusion.scale_ref, bf16[8,48,512]{2,1,0:T(8,128)(2,1)S(1)} %get-tuple-element.30.top_ref, bf16[8,48,512]{2,1,0:T(8,128)(2,1)S(1)} %collective-permute-done.6.bottom_ref, ...), custom_call_target="tpu_custom_call" | custom-call | flops 20999999488 | bytes 4194304 | tf_op jit(solution)/shard_map/windows/pallas_call | solution.py:181
  92.7 0.1 collective-permute-start.7
  92.9 9.8 %collective-permute-done.7 = bf16[8,48,512]{2,1,0:T(8,128)(2,1)S(1)} collective-permute-done((bf16[8,48,512]{2,1,0:T(8,128)(2,1)S(1)}, bf16[8,48,512]{2,1,0:T(8,128)(2,1)S(1)}, u32[]{:S(2)}, u32[]{:S(2)}) %collective-permute-start.7) | collective-permute-done | bytes 393248 | tf_op jit(solution)/shard_map/ppermute | solution.py:23
  102.7 0.0 collective-permute-done.10
  102.7 1.5 %pad_maximum_fusion = bf16[16,128,512]{2,1,0:T(8,128)(2,1)} fusion(bf16[8,128,512]{2,1,0:T(8,128)(2,1)S(1)} %slice_dynamic-update-slice_fusion, bf16[8,128,512]{2,1,0:T(8,128)(2,1)S(1)} %constant_dynamic-update-slice_fusion), kind=kLoop, calls=%fused_computation | loop fusion | flops 1048576 | bytes 4194304 | tf_op jit(solution)/shard_map/concatenate | solution.py:253
  (25 shorter events, 0.2 us)
Async XLA Ops:
  0.0 10.6 %copy-start.5 = (f32[16,31,31]{2,0,1:T(8,128)S(1)}, f32[16,31,31]{2,0,1:T(8,128)}, u32[]{:S(2)}) copy-start(f32[16,31,31]{2,0,1:T(8,128)} %param.19) | copy-start | bytes 184516
  1.6 15.9 %collective-permute-start.1 = (bf16[8,8,512]{2,1,0:T(8,128)(2,1)}, bf16[8,8,512]{2,1,0:T(8,128)(2,1)}, u32[]{:S(2)}, u32[]{:S(2)}) collective-permute-start(bf16[8,8,512]{2,1,0:T(8,128)(2,1)} %get-tuple-element.31), channel_id=1, source_target_pairs={{0,30},{2,0},{4,2},{6,4},{8,6},{10,8},{12,10},{14,12},{16,14},{18,... | collective-permute-start | bytes 196616 | tf_op jit(solution)/shard_map/ppermute | solution.py:23
  7.1 10.4 %collective-permute-start.2 = (bf16[8,8,512]{2,1,0:T(8,128)(2,1)}, bf16[8,8,512]{2,1,0:T(8,128)(2,1)}, u32[]{:S(2)}, u32[]{:S(2)}) collective-permute-start(bf16[8,8,512]{2,1,0:T(8,128)(2,1)} %get-tuple-element.32), channel_id=1, source_target_pairs={{0,31},{1,30},{2,1},{3,0},{4,3},{5,2},{6,5},{7,4},{8,7},{9,6},{10,... | collective-permute-start | bytes 196616 | tf_op jit(solution)/shard_map/ppermute | solution.py:33
  8.7 9.7 %collective-permute-start = (bf16[8,8,512]{2,1,0:T(8,128)(2,1)}, bf16[8,8,512]{2,1,0:T(8,128)(2,1)}, u32[]{:S(2)}, u32[]{:S(2)}) collective-permute-start(bf16[8,8,512]{2,1,0:T(8,128)(2,1)} %get-tuple-element.33), channel_id=1, source_target_pairs={{0,1},{1,0},{2,3},{3,2},{4,5},{5,4},{6,7},{7,6},{8,9},{9,8},{10,11... | collective-permute-start | bytes 196616 | tf_op jit(solution)/shard_map/ppermute | solution.py:23
  10.5 31.2 %collective-permute-start.4 = (bf16[8,32,512]{2,1,0:T(8,128)(2,1)S(1)}, bf16[8,32,512]{2,1,0:T(8,128)(2,1)S(1)}, u32[]{:S(2)}, u32[]{:S(2)}) collective-permute-start(bf16[8,32,512]{2,1,0:T(8,128)(2,1)S(1)} %get-tuple-element.26), channel_id=1, source_target_pairs={{0,30},{2,0},{4,2},{6,4},{8,6},{10,8},{12,10},{14,12},{16,14},{18,... | collective-permute-start | bytes 786440 | tf_op jit(solution)/shard_map/ppermute | solution.py:23
  11.0 5.8 %copy-start.6 = (f32[512]{0:T(512)S(1)}, f32[512]{0:T(512)}, u32[]{:S(2)}) copy-start(f32[512]{0:T(512)} %param.23) | copy-start | bytes 6148
  11.0 5.8 %copy-start.7 = (f32[512]{0:T(512)S(1)}, f32[512]{0:T(512)}, u32[]{:S(2)}) copy-start(f32[512]{0:T(512)} %param.22) | copy-start | bytes 6148
  11.1 8.2 %copy-start.3 = (bf16[512,512]{1,0:T(8,128)(2,1)S(1)}, bf16[512,512]{1,0:T(8,128)(2,1)}, u32[]{:S(2)}) copy-start(bf16[512,512]{1,0:T(8,128)(2,1)} %wproj_ref.7) | copy-start | bytes 1572868
  11.1 8.2 %copy-start.4 = (s32[1,8]{1,0:T(1,128)S(1)}, s32[1,8]{1,0:T(1,128)}, u32[]{:S(2)}) copy-start(s32[1,8]{1,0:T(1,128)} %tissue_ref.7) | copy-start | bytes 100
  19.3 1.6 %copy-start = (bf16[512,2048]{1,0:T(8,128)(2,1)S(1)}, bf16[512,2048]{1,0:T(8,128)(2,1)}, u32[]{:S(2)}) copy-start(bf16[512,2048]{1,0:T(8,128)(2,1)} %wfc1_ref.7) | copy-start | bytes 6291460
  20.9 1.6 %copy-start.2 = (bf16[2048,512]{1,0:T(8,128)(2,1)S(1)}, bf16[2048,512]{1,0:T(8,128)(2,1)}, u32[]{:S(2)}) copy-start(bf16[2048,512]{1,0:T(8,128)(2,1)} %wfc2_ref.7) | copy-start | bytes 6291460
  30.0 11.7 %copy-start.1 = (bf16[512,2048]{1,0:T(8,128)(2,1)S(1)}, bf16[512,2048]{1,0:T(8,128)(2,1)}, u32[]{:S(2)}) copy-start(bf16[512,2048]{1,0:T(8,128)(2,1)} %wfc1_ref.7) | copy-start | bytes 6291460
  30.0 7.4 %collective-permute-start.3 = (bf16[8,8,512]{2,1,0:T(8,128)(2,1)S(1)}, bf16[8,8,512]{2,1,0:T(8,128)(2,1)S(1)}, u32[]{:S(2)}, u32[]{:S(2)}) collective-permute-start(bf16[8,8,512]{2,1,0:T(8,128)(2,1)S(1)} %get-tuple-element.38), channel_id=1, source_target_pairs={{0,3},{1,2},{2,5},{3,4},{4,7},{5,6},{6,9},{7,8},{8,11},{9,10},{10,... | collective-permute-start | bytes 196616 | tf_op jit(solution)/shard_map/ppermute | solution.py:33
  32.8 38.4 %collective-permute-start.6 = (bf16[8,48,512]{2,1,0:T(8,128)(2,1)S(1)}, bf16[8,48,512]{2,1,0:T(8,128)(2,1)S(1)}, u32[]{:S(2)}, u32[]{:S(2)}) collective-permute-start(bf16[8,48,512]{2,1,0:T(8,128)(2,1)S(1)} %get-tuple-element.29), channel_id=1, source_target_pairs={{0,30},{2,0},{4,2},{6,4},{8,6},{10,8},{12,10},{14,12},{16,14},{18,... | collective-permute-start | bytes 1179656 | tf_op jit(solution)/shard_map/ppermute | solution.py:23
  36.6 19.6 %collective-permute-start.8 = (bf16[8,32,512]{2,1,0:T(8,128)(2,1)S(1)}, bf16[8,32,512]{2,1,0:T(8,128)(2,1)S(1)}, u32[]{:S(2)}, u32[]{:S(2)}) collective-permute-start(bf16[8,32,512]{2,1,0:T(8,128)(2,1)S(1)} %get-tuple-element.25), channel_id=1, source_target_pairs={{0,30},{2,0},{4,2},{6,4},{8,6},{10,8},{12,10},{14,12},{16,14},{18,... | collective-permute-start | bytes 786440 | tf_op jit(solution)/shard_map/ppermute | solution.py:23
  36.7 66.0 %collective-permute-start.10 = (bf16[8,8,512]{2,1,0:T(8,128)(2,1)S(1)}, bf16[8,8,512]{2,1,0:T(8,128)(2,1)S(1)}, u32[]{:S(2)}, u32[]{:S(2)}) collective-permute-start(bf16[8,8,512]{2,1,0:T(8,128)(2,1)S(1)} %get-tuple-element.37), channel_id=1, source_target_pairs={{0,2},{2,4},{4,6},{6,8},{8,10},{10,12},{12,14},{14,16},{16,18},{18... | collective-permute-start | bytes 196616 | tf_op jit(solution)/shard_map/ppermute | solution.py:23
  37.4 4.3 %collective-permute-start.11 = (bf16[8,8,512]{2,1,0:T(8,128)(2,1)S(1)}, bf16[8,8,512]{2,1,0:T(8,128)(2,1)S(1)}, u32[]{:S(2)}, u32[]{:S(2)}) collective-permute-start(bf16[8,8,512]{2,1,0:T(8,128)(2,1)S(1)} %slice.62), channel_id=1, source_target_pairs={{0,1},{1,0},{2,3},{3,2},{4,5},{5,4},{6,7},{7,6},{8,9},{9,8},{10,11... | collective-permute-start | bytes 196616 | tf_op jit(solution)/shard_map/ppermute | solution.py:23
  56.2 36.6 %collective-permute-start.5 = (bf16[8,32,512]{2,1,0:T(8,128)(2,1)S(1)}, bf16[8,32,512]{2,1,0:T(8,128)(2,1)S(1)}, u32[]{:S(2)}, u32[]{:S(2)}) collective-permute-start(bf16[8,32,512]{2,1,0:T(8,128)(2,1)S(1)} %get-tuple-element.18), channel_id=1, source_target_pairs={{0,2},{2,4},{4,6},{6,8},{8,10},{10,12},{12,14},{14,16},{16,18},{18... | collective-permute-start | bytes 786440 | tf_op jit(solution)/shard_map/ppermute | solution.py:23
  70.8 31.8 %collective-permute-start.9 = (bf16[8,32,512]{2,1,0:T(8,128)(2,1)S(1)}, bf16[8,32,512]{2,1,0:T(8,128)(2,1)S(1)}, u32[]{:S(2)}, u32[]{:S(2)}) collective-permute-start(bf16[8,32,512]{2,1,0:T(8,128)(2,1)S(1)} %get-tuple-element.20), channel_id=1, source_target_pairs={{0,2},{2,4},{4,6},{6,8},{8,10},{10,12},{12,14},{14,16},{16,18},{18... | collective-permute-start | bytes 786440 | tf_op jit(solution)/shard_map/ppermute | solution.py:23
  92.7 10.0 %collective-permute-start.7 = (bf16[8,48,512]{2,1,0:T(8,128)(2,1)S(1)}, bf16[8,48,512]{2,1,0:T(8,128)(2,1)S(1)}, u32[]{:S(2)}, u32[]{:S(2)}) collective-permute-start(bf16[8,48,512]{2,1,0:T(8,128)(2,1)S(1)} %get-tuple-element.19), channel_id=1, source_target_pairs={{0,2},{2,4},{4,6},{6,8},{8,10},{10,12},{12,14},{14,16},{16,18},{18... | collective-permute-start | bytes 1179656 | tf_op jit(solution)/shard_map/ppermute | solution.py:23

commit v3 on v2

--- a/solution.py
+++ b/solution.py
@@ -135,6 +135,7 @@
     bottom_out_ref,
     triple_ref,
     mixed_ref,
+    raised_ref,
 ):
     w = pl.program_id(0)
     half = SHIFT * WIN
@@ -149,17 +150,27 @@
         triple_ref[at * DIM : (at + 1) * DIM, :] = part.reshape(DIM, TOKENS).astype(jnp.bfloat16)
     triple_ref[2 * DIM :, :] = triple[2 * DIM :]
     ones = jnp.ones((16, TOKENS), jnp.bfloat16)
-    for h in range(HEADS):
+    def score(h):
         at = h * HEAD_DIM
         query = triple_ref[at : at + HEAD_DIM, :]
         key = triple_ref[DIM + at : DIM + at + HEAD_DIM, :]
+        return tn_dot(key, query) * scale_ref[h] + bias_ref[h]
+
+    def soften(scores):
+        highest = jnp.max(scores, axis=0, keepdims=True)
+        return jnp.exp2(scores - highest).astype(jnp.bfloat16)
+
+    def mix(h, raised):
+        at = h * HEAD_DIM
         value = triple_ref[2 * DIM + at : 2 * DIM + at + HEAD_DIM, :]
-        scores = tn_dot(key, query) * scale_ref[h] + bias_ref[h]
-        highest = jnp.max(scores, axis=0, keepdims=True)
-        raised = jnp.exp2(scores - highest).astype(jnp.bfloat16)
         both = nn_dot(jnp.concatenate([value, ones], axis=0), raised)
         mixed = both[:HEAD_DIM] * (1.0 / both[HEAD_DIM : HEAD_DIM + 1])
         mixed_ref[at : at + HEAD_DIM, :] = mixed.astype(jnp.bfloat16)
+
+    for h in range(HEADS):
+        raised_ref[h] = soften(score(h))
+    for h in range(HEADS):
+        mix(h, raised_ref[h])
     keep = tissue_ref[0, first + w].astype(jnp.float32)
     projected = tn_dot(mixed_ref[...], wproj_ref[...])
     branch = layer_norm(projected, norm_ref[0:1, :], norm_ref[1:2, :])
@@ -172,7 +183,7 @@
     bottom_out_ref[...] = final[half:].reshape(SHIFT, WIN, DIM)
 
 
-def run_windows(first, tissue, scale, top, bottom, weights, norms, bias):
+def run_windows(tissue, scale, weights, norms, first, top, bottom, bias):
     count = top.shape[1] // WIN
     smem = pl.BlockSpec(memory_space=pltpu.SMEM)
     whole = pl.BlockSpec(memory_space=pltpu.VMEM)
@@ -187,6 +198,7 @@
         scratch_shapes=[
             pltpu.VMEM((3 * DIM, TOKENS), jnp.bfloat16),
             pltpu.VMEM((DIM, TOKENS), jnp.bfloat16),
+            pltpu.VMEM((HEADS, TOKENS, TOKENS), jnp.bfloat16),
         ],
         compiler_params=pltpu.CompilerParams(
             vmem_limit_bytes=32 * 2**20, dimension_semantics=("arbitrary",)
@@ -224,32 +236,33 @@
     norms = jnp.stack([norm1_gain, norm1_bias, norm2_gain, norm2_bias])
     inner_bias, last_bias = build_bias(edges, bias_table)
     windows = tile_cols // WIN
-    bounds = [windows, windows - 1, windows * 5 // 8, windows // 4, 0]
-    parts = [(lo, hi) for hi, lo in zip(bounds, bounds[1:]) if hi > lo]
+    middle = windows // 2 * WIN
+    right = tile_cols - WIN
     side = shifted(crop[SHIFT:, :SHIFT], "col", -1)
     corner = shifted_both(crop[:SHIFT, :SHIFT], -1)
-    tops, bottoms = ([], [])
-    for lo, hi in parts:
-        start, stop = (lo * WIN + SHIFT, hi * WIN + SHIFT)
-        top = crop[SHIFT:, start : min(stop, tile_cols)]
-        bottom = shifted(crop[:SHIFT, start : min(stop, tile_cols)], "row", -1)
-        if stop > tile_cols:
-            top = jnp.concatenate([top, side], axis=1)
-            bottom = jnp.concatenate([bottom, corner], axis=1)
-        tops.append(top)
-        bottoms.append(bottom)
-    own, above = ([], [])
-    for (lo, hi), top, bottom in zip(parts, tops, bottoms):
-        bias = last_bias if hi == windows else inner_bias
-        top, bottom = run_windows(lo, tissue, scale, top, bottom, weights, norms, bias)
-        if hi == windows:
-            from_left = shifted(top[:, -SHIFT:], "col", 1)
-            from_corner = shifted_both(bottom[:, -SHIFT:], 1)
-            top, bottom = (top[:, :-SHIFT], bottom[:, :-SHIFT])
-        own.insert(0, top)
-        above.insert(0, shifted(bottom, "row", 1))
-    upper = jnp.concatenate([from_corner] + above, axis=1)
-    lower = jnp.concatenate([from_left] + own, axis=1)
+    split = middle + SHIFT
+    below_right = shifted(crop[:SHIFT, split:], "row", -1)
+    below_left = shifted(crop[:SHIFT, SHIFT:split], "row", -1)
+    run = functools.partial(run_windows, tissue, scale, weights, norms)
+    end = right + SHIFT - split
+    top_end, bottom_end = run(
+        windows - 1,
+        jnp.concatenate([crop[SHIFT:, right + SHIFT :], side], axis=1),
+        jnp.concatenate([below_right[:, end:], corner], axis=1),
+        last_bias,
+    )
+    from_left = shifted(top_end[:, SHIFT:], "col", 1)
+    from_corner = shifted_both(bottom_end[:, SHIFT:], 1)
+    top_right, bottom_right = run(
+        windows // 2, crop[SHIFT:, split : right + SHIFT], below_right[:, :end], inner_bias
+    )
+    above_right = shifted(
+        jnp.concatenate([bottom_right, bottom_end[:, :SHIFT]], axis=1), "row", 1
+    )
+    top_left, bottom_left = run(0, crop[SHIFT:, SHIFT:split], below_left, inner_bias)
+    above_left = shifted(bottom_left, "row", 1)
+    upper = jnp.concatenate([from_corner, above_left, above_right], axis=1)
+    lower = jnp.concatenate([from_left, top_left, top_right, top_end[:, :SHIFT]], axis=1)
     return jnp.concatenate([upper, lower], axis=0)
 
 

time: 105 us -> 83.1 us (0.79)
  Pallas kernels: 61.1 us -> 40 us
  starting transfers between devices: 15.6 us -> 10.7 us
  local copies, waits for them, and re-layouts: 9.77 us -> 12.2 us
  waiting for transfers between devices: 12.7 us -> 14.9 us
    pallas_call x4 -> x3, Pallas kernels: 58.1 us -> 37 us  [run_windows(): pl.pallas_call(functools.partial(window_kernel, first), grid=(count,), ou...]
    ppermute x2, waiting for transfers between devices: 0.23 us -> 14.8 us  [shifted_both(): return lax.ppermute(x, ('row', 'col'), pairs)]
    ppermute x10 -> x6, waiting for transfers between devices: 12.5 us -> 0.02 us  [shifted(): return lax.ppermute(x, axis, [(i, (i + by) % count) for i in range(count)])]
    ppermute x10 -> x6, starting transfers between devices: 12.3 us -> 5.91 us  [shifted(): return lax.ppermute(x, axis, [(i, (i + by) % count) for i in range(count)])]
    slice x5 -> x8, local copies, waits for them, and re-layouts: 4.08 us -> 6.62 us  [the longest x1 2.09 us: on_device(): below_left = shifted(crop[:SHIFT, SHIFT:split], 'row', -1)]
    ppermute x2, starting transfers between devices: 3.23 us -> 4.84 us  [shifted_both(): return lax.ppermute(x, ('row', 'col'), pairs)]
    unnamed x25 -> x17, local copies, waits for them, and re-layouts: 5.07 us -> 4.98 us
  transfers between devices with their start and end apart: 12 -> 8, of which waited for: 3 -> 1; matrix products, arithmetic and copies ran while one was open for 8% -> 13% of each run, Pallas kernels for 59% -> 26%
where the time goes in v3:
time: 83.1 us; the launch traced here: 82.7 us
  Pallas kernels  40 us (48%)
  waiting for transfers between devices  14.9 us (18%)
  local copies, waits for them, and re-layouts  12.2 us (15%)
  starting transfers between devices  10.7 us (13%)
  other arithmetic  4.67 us (6%)
    pallas_call x3, Pallas kernels, run_windows(): pl.pallas_call(functools.partial(window_kernel, first), grid=(count,), ou...  37 us
    ppermute x2, waiting for transfers between devices, shifted_both(): return lax.ppermute(x, ('row', 'col'), pairs)  14.8 us
    ppermute x6, starting transfers between devices, shifted(): return lax.ppermute(x, axis, [(i, (i + by) % count) for i in range(count)])  5.91 us
    unnamed x17, local copies, waits for them, and re-layouts  4.98 us
    ppermute x2, starting transfers between devices, shifted_both(): return lax.ppermute(x, ('row', 'col'), pairs)  4.84 us
    pallas_call x1, Pallas kernels, build_bias(): pl.pallas_call(bias_kernel, out_shape=[jax.ShapeDtypeStruct((HEADS, TOKEN...  3.01 us
    slice x1, local copies, waits for them, and re-layouts, on_device(): below_left = shifted(crop[:SHIFT, SHIFT:split], 'row', -1)  2.09 us
    slice x1, local copies, waits for them, and re-layouts, on_device(): below_right = shifted(crop[:SHIFT, split:], 'row', -1)  1.82 us
  transfers between devices with their start and end apart: 8, of which 1 were waited for; matrix products, arithmetic and copies ran while one was open for 13% of the time, Pallas kernels for 26%

profile of v3, /device:TPU:0, one launch (start us, length us, event | category | flops | bytes accessed | tf_op | source)
XLA Modules:
  0.0 82.7 jit_solution(18443204054906355025)
XLA Ops:
  0.0 1.6 %fusion.1 = (bf16[8,8,512]{2,1,0:T(8,128)(2,1)}, bf16[8,8,512]{2,1,0:T(8,128)(2,1)}, bf16[8,8,512]{2,1,0:T(8,128)(2,1)}) fusion(bf16[16,128,512]{2,1,0:T(8,128)(2,1)} %param.12), kind=kLoop, calls=%fused_computation.11 | loop fusion | bytes 393216 | tf_op jit(solution)/shard_map/slice | solution.py:242
  1.6 2.9 %collective-permute-start = (bf16[8,8,512]{2,1,0:T(8,128)(2,1)}, bf16[8,8,512]{2,1,0:T(8,128)(2,1)}, u32[]{:S(2)}, u32[]{:S(2)}) collective-permute-start(bf16[8,8,512]{2,1,0:T(8,128)(2,1)} %get-tuple-element.24), channel_id=1, source_target_pairs={{0,1},{1,0},{2,3},{3,2},{4,5},{5,4},{6,7},{7,6},{8,9},{9,8},{10,11... | collective-permute-start | bytes 196616 | tf_op jit(solution)/shard_map/ppermute | solution.py:23
  4.6 3.7 %collective-permute-start.2 = (bf16[8,8,512]{2,1,0:T(8,128)(2,1)}, bf16[8,8,512]{2,1,0:T(8,128)(2,1)}, u32[]{:S(2)}, u32[]{:S(2)}) collective-permute-start(bf16[8,8,512]{2,1,0:T(8,128)(2,1)} %get-tuple-element.23), channel_id=1, source_target_pairs={{0,31},{1,30},{2,1},{3,0},{4,3},{5,2},{6,5},{7,4},{8,7},{9,6},{10,... | collective-permute-start | bytes 196616 | tf_op jit(solution)/shard_map/ppermute | solution.py:33
  8.3 1.8 %slice.47 = bf16[8,56,512]{2,1,0:T(8,128)(2,1)} slice(bf16[16,128,512]{2,1,0:T(8,128)(2,1)} %param.12), slice={[0:8], [72:128], [0:512]} | slice | bytes 917504 | tf_op jit(solution)/shard_map/slice | solution.py:244
  10.1 1.1 %collective-permute-start.1 = (bf16[8,56,512]{2,1,0:T(8,128)(2,1)}, bf16[8,56,512]{2,1,0:T(8,128)(2,1)S(1)}, u32[]{:S(2)}, u32[]{:S(2)}) collective-permute-start(bf16[8,56,512]{2,1,0:T(8,128)(2,1)} %slice.47), channel_id=1, source_target_pairs={{0,30},{2,0},{4,2},{6,4},{8,6},{10,8},{12,10},{14,12},{16,14},{18,... | collective-permute-start | bytes 1376264 | tf_op jit(solution)/shard_map/ppermute | solution.py:23
  11.2 2.1 %fusion = (bf16[8,64,512]{2,1,0:T(8,128)(2,1)}, bf16[8,64,512]{2,1,0:T(8,128)(2,1)S(1)}) fusion(bf16[16,128,512]{2,1,0:T(8,128)(2,1)} %param.12), kind=kLoop, calls=%fused_computation.10 | loop fusion | bytes 2097152 | tf_op jit(solution)/shard_map/slice | solution.py:245
  13.3 0.0 collective-permute-start.4
  13.3 0.0 copy-done.5
  13.3 0.1 pad_slice_fusion
  13.5 0.1 add_convert_fusion.edge_ref
  13.5 1.0 %slice.55.top_ref = bf16[8,48,512]{2,1,0:T(8,128)(2,1)S(1)} slice(bf16[16,128,512]{2,1,0:T(8,128)(2,1)} %param.12), slice={[8:16], [72:120], [0:512]} | slice | bytes 786432 | tf_op jit(solution)/shard_map/slice | solution.py:257
  14.6 0.1 copy.17
  14.7 0.0 copy-start.6
  14.7 0.0 copy-start.7
  14.7 0.2 reshape.6.low_ref
  14.8 0.1 copy.18
  14.9 0.2 reshape.7.high_ref
  15.1 0.0 copy-start.4
  15.1 1.8 %copy.16 = bf16[512,1536]{0,1:T(8,128)(2,1)S(1)} copy(bf16[512,1536]{1,0:T(8,128)(2,1)} %param.14) | data formatting | bytes 3145728 | tf_op args[2]
  16.9 3.0 %bias.1 = (f32[16,256,256]{2,1,0:T(8,128)S(1)}, f32[16,256,256]{2,1,0:T(8,128)S(1)}) custom-call(s32[2]{0:T(128)S(1)} %add_convert_fusion.edge_ref, f32[16,512]{1,0:T(8,128)S(1)} %reshape.6.low_ref, f32[16,512]{1,0:T(8,128)S(1)} %reshape.7.high_ref), custom_call_target="tpu_custom_call" | custom-call | flops 4194304 | bytes 20971520 | tf_op jit(solution)/shard_map/bias/pallas_call | solution.py:90
  19.9 0.7 exponential_multiply_fusion.scale_ref
  20.6 0.0 copy-done.6
  20.6 0.0 copy-done.7
  20.6 0.7 pad_maximum_fusion.3.norm_ref
  21.3 0.0 collective-permute-done
  21.3 0.9 %pad_maximum_fusion.1.top_ref = bf16[8,16,512]{2,1,0:T(8,128)(2,1)S(1)} fusion(bf16[8,8,512]{2,1,0:T(8,128)(2,1)} %collective-permute-done, bf16[8,8,512]{2,1,0:T(8,128)(2,1)} %get-tuple-element.25), kind=kLoop, calls=%fused_computation.4 | loop fusion | flops 262144 | bytes 262144 | tf_op jit(solution)/shard_map/concatenate | solution.py:250
  22.2 0.0 collective-permute-done.1
  22.2 0.0 copy-done.3
  22.3 0.0 copy-done.4
  22.3 0.0 copy-start
  22.3 1.6 %copy-done = bf16[512,2048]{1,0:T(8,128)(2,1)S(1)} copy-done((bf16[512,2048]{1,0:T(8,128)(2,1)S(1)}, bf16[512,2048]{1,0:T(8,128)(2,1)}, u32[]{:S(2)}) %copy-start) | copy-done | bytes 2097176
  23.9 1.6 %copy-done.2 = bf16[2048,512]{1,0:T(8,128)(2,1)S(1)} copy-done((bf16[2048,512]{1,0:T(8,128)(2,1)S(1)}, bf16[2048,512]{1,0:T(8,128)(2,1)}, u32[]{:S(2)}) %copy-start.2) | copy-done | bytes 2097176
  25.4 13.6 %windows.5 = (bf16[8,48,512]{2,1,0:T(8,128)(2,1)S(1)}, bf16[8,48,512]{2,1,0:T(8,128)(2,1)S(1)}) custom-call(s32[1,8]{1,0:T(1,128)S(1)} %copy-done.4, f32[16]{0:T(128)S(1)} %exponential_multiply_fusion.scale_ref, bf16[8,48,512]{2,1,0:T(8,128)(2,1)S(1)} %slice.55.top_ref, bf16[8,48,512]{2,1,0:T(8,128)(2,1)S(1)} %slice.61.bottom_ref, ...), custom_call_target="tpu_custom_call" | custom-call | flops 20999999488 | bytes 4194304 | tf_op jit(solution)/shard_map/windows/pallas_call | solution.py:192
  39.1 0.0 collective-permute-done.2
  39.1 0.8 %pad_maximum_fusion.2.bottom_ref = bf16[8,16,512]{2,1,0:T(8,128)(2,1)S(1)} fusion(bf16[8,8,512]{2,1,0:T(8,128)(2,1)} %collective-permute-done.2, bf16[8,8,512]{2,1,0:T(8,128)(2,1)S(1)} %slice.60), kind=kLoop, calls=%fused_computation.5 | loop fusion | flops 262144 | bytes 262144 | tf_op jit(solution)/shard_map/concatenate | solution.py:251
  40.0 0.0 copy-done.1
  40.0 4.9 %windows.3 = (bf16[8,16,512]{2,1,0:T(8,128)(2,1)S(1)}, bf16[8,16,512]{2,1,0:T(8,128)(2,1)S(1)}) custom-call(s32[1,8]{1,0:T(1,128)S(1)} %copy-done.4, f32[16]{0:T(128)S(1)} %exponential_multiply_fusion.scale_ref, bf16[8,16,512]{2,1,0:T(8,128)(2,1)S(1)} %pad_maximum_fusion.1.top_ref, bf16[8,16,512]{2,1,0:T(8,128)(2,1)S(1)} %pad_maximum_fusion.2.bottom_ref, ...), custom_call_target="tpu_custom_call" | custom-call | flops 7000000000 | bytes 4194304 | tf_op jit(solution)/shard_map/windows/pallas_call | solution.py:192
  45.0 0.0 collective-permute-done.4.bottom_ref
  45.0 18.4 %windows.4 = (bf16[8,64,512]{2,1,0:T(8,128)(2,1)S(1)}, bf16[8,64,512]{2,1,0:T(8,128)(2,1)S(1)}) custom-call(s32[1,8]{1,0:T(1,128)S(1)} %copy-done.4, f32[16]{0:T(128)S(1)} %exponential_multiply_fusion.scale_ref, bf16[8,64,512]{2,1,0:T(8,128)(2,1)S(1)} %get-tuple-element.22.top_ref, bf16[8,64,512]{2,1,0:T(8,128)(2,1)} %collective-permute-done.4.bottom_ref, ...), custom_call_target="tpu_custom_call" | custom-call | flops 28000000000 | bytes 4194304 | tf_op jit(solution)/shard_map/windows/pallas_call | solution.py:192
  63.3 0.5 collective-permute-start.5
  63.9 0.7 collective-permute-start.6
  64.6 1.2 %collective-permute-start.3 = (bf16[8,8,512]{2,1,0:T(8,128)(2,1)S(1)}, bf16[8,8,512]{2,1,0:T(8,128)(2,1)S(1)}, u32[]{:S(2)}, u32[]{:S(2)}) collective-permute-start(bf16[8,8,512]{2,1,0:T(8,128)(2,1)S(1)} %get-tuple-element.28), channel_id=1, source_target_pairs={{0,3},{1,2},{2,5},{3,4},{4,7},{5,6},{6,9},{7,8},{8,11},{9,10},{10,... | collective-permute-start | bytes 196616 | tf_op jit(solution)/shard_map/ppermute | solution.py:33
  65.8 0.6 collective-permute-start.7
  66.4 14.8 %collective-permute-done.3 = bf16[8,8,512]{2,1,0:T(8,128)(2,1)S(1)} collective-permute-done((bf16[8,8,512]{2,1,0:T(8,128)(2,1)S(1)}, bf16[8,8,512]{2,1,0:T(8,128)(2,1)S(1)}, u32[]{:S(2)}, u32[]{:S(2)}) %collective-permute-start.3) | collective-permute-done | bytes 65568 | tf_op jit(solution)/shard_map/ppermute | solution.py:33
  81.2 0.0 collective-permute-done.7
  81.2 0.0 collective-permute-done.6
  81.2 0.0 collective-permute-done.5
  81.2 1.4 %maximum_maximum_fusion = bf16[16,128,512]{2,1,0:T(8,128)(2,1)} fusion(bf16[8,8,512]{2,1,0:T(8,128)(2,1)S(1)} %get-tuple-element.31, bf16[8,48,512]{2,1,0:T(8,128)(2,1)S(1)} %get-tuple-element.20, bf16[8,64,512]{2,1,0:T(8,128)(2,1)S(1)} %get-tuple-element.19, bf16[8,8,512]{2,1,0:T(8,128)(2,1)S(1)} %collective-permute-done.7, ...), kind=kLoop, calls=%fused_computation | loop fusion | flops 14680064 | bytes 4194304 | tf_op jit(solution)/shard_map/concatenate | solution.py:266
  (10 shorter events, 0.1 us)
Async XLA Ops:
  0.0 13.3 %copy-start.5 = (f32[16,31,31]{2,0,1:T(8,128)S(1)}, f32[16,31,31]{2,0,1:T(8,128)}, u32[]{:S(2)}) copy-start(f32[16,31,31]{2,0,1:T(8,128)} %param.19) | copy-start | bytes 184516
  1.6 19.7 %collective-permute-start = (bf16[8,8,512]{2,1,0:T(8,128)(2,1)}, bf16[8,8,512]{2,1,0:T(8,128)(2,1)}, u32[]{:S(2)}, u32[]{:S(2)}) collective-permute-start(bf16[8,8,512]{2,1,0:T(8,128)(2,1)} %get-tuple-element.24), channel_id=1, source_target_pairs={{0,1},{1,0},{2,3},{3,2},{4,5},{5,4},{6,7},{7,6},{8,9},{9,8},{10,11... | collective-permute-start | bytes 196616 | tf_op jit(solution)/shard_map/ppermute | solution.py:23
  4.6 34.5 %collective-permute-start.2 = (bf16[8,8,512]{2,1,0:T(8,128)(2,1)}, bf16[8,8,512]{2,1,0:T(8,128)(2,1)}, u32[]{:S(2)}, u32[]{:S(2)}) collective-permute-start(bf16[8,8,512]{2,1,0:T(8,128)(2,1)} %get-tuple-element.23), channel_id=1, source_target_pairs={{0,31},{1,30},{2,1},{3,0},{4,3},{5,2},{6,5},{7,4},{8,7},{9,6},{10,... | collective-permute-start | bytes 196616 | tf_op jit(solution)/shard_map/ppermute | solution.py:33
  10.1 12.1 %collective-permute-start.1 = (bf16[8,56,512]{2,1,0:T(8,128)(2,1)}, bf16[8,56,512]{2,1,0:T(8,128)(2,1)S(1)}, u32[]{:S(2)}, u32[]{:S(2)}) collective-permute-start(bf16[8,56,512]{2,1,0:T(8,128)(2,1)} %slice.47), channel_id=1, source_target_pairs={{0,30},{2,0},{4,2},{6,4},{8,6},{10,8},{12,10},{14,12},{16,14},{18,... | collective-permute-start | bytes 1376264 | tf_op jit(solution)/shard_map/ppermute | solution.py:23
  13.3 31.7 %collective-permute-start.4 = (bf16[8,64,512]{2,1,0:T(8,128)(2,1)}, bf16[8,64,512]{2,1,0:T(8,128)(2,1)}, u32[]{:S(2)}, u32[]{:S(2)}) collective-permute-start(bf16[8,64,512]{2,1,0:T(8,128)(2,1)} %get-tuple-element.21), channel_id=1, source_target_pairs={{0,30},{2,0},{4,2},{6,4},{8,6},{10,8},{12,10},{14,12},{16,14},{18,... | collective-permute-start | bytes 1572872 | tf_op jit(solution)/shard_map/ppermute | solution.py:23
  14.7 5.9 %copy-start.6 = (f32[512]{0:T(512)S(1)}, f32[512]{0:T(512)}, u32[]{:S(2)}) copy-start(f32[512]{0:T(512)} %param.23) | copy-start | bytes 6148
  14.7 5.9 %copy-start.7 = (f32[512]{0:T(512)S(1)}, f32[512]{0:T(512)}, u32[]{:S(2)}) copy-start(f32[512]{0:T(512)} %param.22) | copy-start | bytes 6148
  15.1 7.2 %copy-start.3 = (bf16[512,512]{1,0:T(8,128)(2,1)S(1)}, bf16[512,512]{1,0:T(8,128)(2,1)}, u32[]{:S(2)}) copy-start(bf16[512,512]{1,0:T(8,128)(2,1)} %wproj_ref.5) | copy-start | bytes 1572868
  15.1 7.2 %copy-start.4 = (s32[1,8]{1,0:T(1,128)S(1)}, s32[1,8]{1,0:T(1,128)}, u32[]{:S(2)}) copy-start(s32[1,8]{1,0:T(1,128)} %tissue_ref.5) | copy-start | bytes 100
  22.3 1.6 %copy-start = (bf16[512,2048]{1,0:T(8,128)(2,1)S(1)}, bf16[512,2048]{1,0:T(8,128)(2,1)}, u32[]{:S(2)}) copy-start(bf16[512,2048]{1,0:T(8,128)(2,1)} %wfc1_ref.5) | copy-start | bytes 6291460
  23.9 1.6 %copy-start.2 = (bf16[2048,512]{1,0:T(8,128)(2,1)S(1)}, bf16[2048,512]{1,0:T(8,128)(2,1)}, u32[]{:S(2)}) copy-start(bf16[2048,512]{1,0:T(8,128)(2,1)} %wfc2_ref.5) | copy-start | bytes 6291460
  25.4 14.5 %copy-start.1 = (bf16[512,2048]{1,0:T(8,128)(2,1)S(1)}, bf16[512,2048]{1,0:T(8,128)(2,1)}, u32[]{:S(2)}) copy-start(bf16[512,2048]{1,0:T(8,128)(2,1)} %wfc1_ref.5) | copy-start | bytes 6291460
  63.3 17.9 %collective-permute-start.5 = (bf16[8,64,512]{2,1,0:T(8,128)(2,1)S(1)}, bf16[8,64,512]{2,1,0:T(8,128)(2,1)S(1)}, u32[]{:S(2)}, u32[]{:S(2)}) collective-permute-start(bf16[8,64,512]{2,1,0:T(8,128)(2,1)S(1)} %get-tuple-element.16), channel_id=1, source_target_pairs={{0,2},{2,4},{4,6},{6,8},{8,10},{10,12},{12,14},{14,16},{16,18},{18... | collective-permute-start | bytes 1572872 | tf_op jit(solution)/shard_map/ppermute | solution.py:23
  63.9 17.3 %collective-permute-start.6 = (bf16[8,56,512]{2,1,0:T(8,128)(2,1)S(1)}, bf16[8,56,512]{2,1,0:T(8,128)(2,1)S(1)}, u32[]{:S(2)}, u32[]{:S(2)}) collective-permute-start(bf16[8,56,512]{2,1,0:T(8,128)(2,1)S(1)} %pad_maximum_fusion), channel_id=1, source_target_pairs={{0,2},{2,4},{4,6},{6,8},{8,10},{10,12},{12,14},{14,16},{16,18},{18... | collective-permute-start | bytes 1376264 | tf_op jit(solution)/shard_map/ppermute | solution.py:23
  64.6 16.6 %collective-permute-start.3 = (bf16[8,8,512]{2,1,0:T(8,128)(2,1)S(1)}, bf16[8,8,512]{2,1,0:T(8,128)(2,1)S(1)}, u32[]{:S(2)}, u32[]{:S(2)}) collective-permute-start(bf16[8,8,512]{2,1,0:T(8,128)(2,1)S(1)} %get-tuple-element.28), channel_id=1, source_target_pairs={{0,3},{1,2},{2,5},{3,4},{4,7},{5,6},{6,9},{7,8},{8,11},{9,10},{10,... | collective-permute-start | bytes 196616 | tf_op jit(solution)/shard_map/ppermute | solution.py:33
  65.8 15.5 %collective-permute-start.7 = (bf16[8,8,512]{2,1,0:T(8,128)(2,1)S(1)}, bf16[8,8,512]{2,1,0:T(8,128)(2,1)S(1)}, u32[]{:S(2)}, u32[]{:S(2)}) collective-permute-start(bf16[8,8,512]{2,1,0:T(8,128)(2,1)S(1)} %get-tuple-element.30), channel_id=1, source_target_pairs={{0,1},{1,0},{2,3},{3,2},{4,5},{5,4},{6,7},{7,6},{8,9},{9,8},{10,11... | collective-permute-start | bytes 196616 | tf_op jit(solution)/shard_map/ppermute | solution.py:23

commit v4 on v3

--- a/solution.py
+++ b/solution.py
@@ -121,6 +121,7 @@
 
 def window_kernel(
     first,
+    unused,
     tissue_ref,
     scale_ref,
     top_ref,
@@ -131,12 +132,9 @@
     wfc2_ref,
     norm_ref,
     bias_ref,
-    top_out_ref,
-    bottom_out_ref,
-    triple_ref,
-    mixed_ref,
-    raised_ref,
+    *refs,
 ):
+    top_out_ref, bottom_out_ref, triple_ref, mixed_ref, raised_ref = refs[unused:]
     w = pl.program_id(0)
     half = SHIFT * WIN
     x = jnp.concatenate(
@@ -183,17 +181,19 @@
     bottom_out_ref[...] = final[half:].reshape(SHIFT, WIN, DIM)
 
 
-def run_windows(tissue, scale, weights, norms, first, top, bottom, bias):
+def run_windows(tissue, scale, weights, norms, first, top, bottom, bias, after=()):
     count = top.shape[1] // WIN
     smem = pl.BlockSpec(memory_space=pltpu.SMEM)
     whole = pl.BlockSpec(memory_space=pltpu.VMEM)
     tile = pl.BlockSpec((SHIFT, WIN, DIM), lambda w: (0, w, 0))
     half = jax.ShapeDtypeStruct(top.shape, jnp.bfloat16)
     return pl.pallas_call(
-        functools.partial(window_kernel, first),
+        functools.partial(window_kernel, first, len(after)),
         grid=(count,),
         out_shape=[half, half],
-        in_specs=[smem, smem, tile, tile] + [whole] * 6,
+        in_specs=[smem, smem, tile, tile]
+        + [whole] * 6
+        + [pl.BlockSpec(memory_space=pl.ANY)] * len(after),
         out_specs=[tile, tile],
         scratch_shapes=[
             pltpu.VMEM((3 * DIM, TOKENS), jnp.bfloat16),
@@ -207,7 +207,7 @@
             flops=count * 7 * 10**9, bytes_accessed=4 * 2**20, transcendentals=count * 2**20
         ),
         name="windows",
-    )(tissue, scale, top, bottom, *weights, norms, bias)
+    )(tissue, scale, top, bottom, *weights, norms, bias, *after)
 
 
 def on_device(
@@ -259,10 +259,23 @@
     above_right = shifted(
         jnp.concatenate([bottom_right, bottom_end[:, :SHIFT]], axis=1), "row", 1
     )
-    top_left, bottom_left = run(0, crop[SHIFT:, SHIFT:split], below_left, inner_bias)
-    above_left = shifted(bottom_left, "row", 1)
-    upper = jnp.concatenate([from_corner, above_left, above_right], axis=1)
-    lower = jnp.concatenate([from_left, top_left, top_right, top_end[:, :SHIFT]], axis=1)
+    cuts = [windows // 2, windows // 4, windows // 8, 0]
+    sent = [(above_right, from_left, from_corner)]
+    own, above = ([top_right, top_end[:, :SHIFT]], [above_right])
+    for step, (hi, lo) in enumerate(zip(cuts, cuts[1:])):
+        start, stop = (lo * WIN, hi * WIN)
+        top, bottom = run(
+            lo,
+            crop[SHIFT:, start + SHIFT : stop + SHIFT],
+            below_left[:, start:stop],
+            inner_bias,
+            sent[step - 1] + (own[0],) if step >= 1 else (),
+        )
+        own.insert(0, top)
+        above.insert(0, shifted(bottom, "row", 1))
+        sent.append((above[0],))
+    upper = jnp.concatenate([from_corner] + above, axis=1)
+    lower = jnp.concatenate([from_left] + own, axis=1)
     return jnp.concatenate([upper, lower], axis=0)
 
 

time: 83.1 us -> 84 us (1.011)
  local copies, waits for them, and re-layouts: 12.2 us -> 17.9 us
  waiting for transfers between devices: 14.9 us -> 10.8 us
  other arithmetic: 4.67 us -> 2.52 us
  Pallas kernels: 40 us -> 40.9 us
    ppermute x2, waiting for transfers between devices: 14.8 us -> 0.01 us  [shifted_both(): return lax.ppermute(x, ('row', 'col'), pairs)]
    ppermute x6 -> x8, waiting for transfers between devices: 0.02 us -> 10.8 us  [shifted(): return lax.ppermute(x, axis, [(i, (i + by) % count) for i in range(count)])]
    slice x0 -> x4, local copies, waits for them, and re-layouts: none -> 3.93 us  [the longest x2 1.96 us: on_device(): crop[SHIFT:, start + SHIFT:stop + SHIFT]]
    slice x1, local copies, waits for them, and re-layouts: 0.03 us -> 1.02 us  [on_device(): below_right[:, :end]]
    pallas_call x3 -> x5, Pallas kernels: 37 us -> 37.9 us  [run_windows(): pl.pallas_call(functools.partial(window_kernel, first, len(after)), grid=...]
    concatenate x1, other arithmetic: 0.85 us -> 0.01 us  [on_device(): jnp.concatenate([below_right[:, end:], corner], axis=1)]
    ppermute x6 -> x8, starting transfers between devices: 5.91 us -> 6.15 us  [shifted(): return lax.ppermute(x, axis, [(i, (i + by) % count) for i in range(count)])]
    unnamed x17 -> x34, local copies, waits for them, and re-layouts: 4.98 us -> 5.07 us
  transfers between devices with their start and end apart: 8 -> 10, of which waited for: 1 -> 3; matrix products, arithmetic and copies ran while one was open for 13% -> 17% of each run, Pallas kernels for 26% -> 43%
where the time goes in v4:
time: 84 us; the launch traced here: 83.4 us
  Pallas kernels  40.9 us (49%)
  local copies, waits for them, and re-layouts  17.9 us (21%)
  starting transfers between devices  10.9 us (13%)
  waiting for transfers between devices  10.8 us (13%)
  other arithmetic  2.52 us (3%)
    pallas_call x5, Pallas kernels, run_windows(): pl.pallas_call(functools.partial(window_kernel, first, len(after)), grid=...  37.9 us
    ppermute x8, waiting for transfers between devices, shifted(): return lax.ppermute(x, axis, [(i, (i + by) % count) for i in range(count)])  10.8 us
    ppermute x8, starting transfers between devices, shifted(): return lax.ppermute(x, axis, [(i, (i + by) % count) for i in range(count)])  6.15 us
    unnamed x34, local copies, waits for them, and re-layouts  5.07 us
    ppermute x2, starting transfers between devices, shifted_both(): return lax.ppermute(x, ('row', 'col'), pairs)  4.73 us
    pallas_call x1, Pallas kernels, build_bias(): pl.pallas_call(bias_kernel, out_shape=[jax.ShapeDtypeStruct((HEADS, TOKEN...  3.03 us
    slice x2, local copies, waits for them, and re-layouts, on_device(): crop[SHIFT:, start + SHIFT:stop + SHIFT]  1.96 us
    slice x2, local copies, waits for them, and re-layouts, on_device(): below_left[:, start:stop]  1.96 us
  transfers between devices with their start and end apart: 10, of which 3 were waited for; matrix products, arithmetic and copies ran while one was open for 17% of the time, Pallas kernels for 43%

profile of v4, /device:TPU:0, one launch (start us, length us, event | category | flops | bytes accessed | tf_op | source)
XLA Modules:
  0.0 83.4 jit_solution(4498336283113728878)
XLA Ops:
  0.0 1.6 %fusion.1 = (bf16[8,8,512]{2,1,0:T(8,128)(2,1)S(1)}, bf16[8,8,512]{2,1,0:T(8,128)(2,1)}, bf16[8,8,512]{2,1,0:T(8,128)(2,1)S(1)}) fusion(bf16[16,128,512]{2,1,0:T(8,128)(2,1)} %param.12), kind=kLoop, calls=%fused_computation.22 | loop fusion | bytes 393216 | tf_op jit(solution)/shard_map/slice | solution.py:242
  1.6 2.9 %collective-permute-start = (bf16[8,8,512]{2,1,0:T(8,128)(2,1)}, bf16[8,8,512]{2,1,0:T(8,128)(2,1)}, u32[]{:S(2)}, u32[]{:S(2)}) collective-permute-start(bf16[8,8,512]{2,1,0:T(8,128)(2,1)} %get-tuple-element.32), channel_id=1, source_target_pairs={{0,1},{1,0},{2,3},{3,2},{4,5},{5,4},{6,7},{7,6},{8,9},{9,8},{10,11... | collective-permute-start | bytes 196616 | tf_op jit(solution)/shard_map/ppermute | solution.py:23
  4.5 3.7 %collective-permute-start.2 = (bf16[8,8,512]{2,1,0:T(8,128)(2,1)S(1)}, bf16[8,8,512]{2,1,0:T(8,128)(2,1)S(1)}, u32[]{:S(2)}, u32[]{:S(2)}) collective-permute-start(bf16[8,8,512]{2,1,0:T(8,128)(2,1)S(1)} %get-tuple-element.31), channel_id=1, source_target_pairs={{0,31},{1,30},{2,1},{3,0},{4,3},{5,2},{6,5},{7,4},{8,7},{9,6},{10,... | collective-permute-start | bytes 196616 | tf_op jit(solution)/shard_map/ppermute | solution.py:33
  8.2 1.8 %slice.62 = bf16[8,56,512]{2,1,0:T(8,128)(2,1)} slice(bf16[16,128,512]{2,1,0:T(8,128)(2,1)} %param.12), slice={[0:8], [72:128], [0:512]} | slice | bytes 917504 | tf_op jit(solution)/shard_map/slice | solution.py:244
  10.0 1.1 %collective-permute-start.1 = (bf16[8,56,512]{2,1,0:T(8,128)(2,1)}, bf16[8,56,512]{2,1,0:T(8,128)(2,1)}, u32[]{:S(2)}, u32[]{:S(2)}) collective-permute-start(bf16[8,56,512]{2,1,0:T(8,128)(2,1)} %slice.62), channel_id=1, source_target_pairs={{0,30},{2,0},{4,2},{6,4},{8,6},{10,8},{12,10},{14,12},{16,14},{18,... | collective-permute-start | bytes 1376264 | tf_op jit(solution)/shard_map/ppermute | solution.py:23
  11.2 1.9 %slice.69 = bf16[8,64,512]{2,1,0:T(8,128)(2,1)} slice(bf16[16,128,512]{2,1,0:T(8,128)(2,1)} %param.12), slice={[0:8], [8:72], [0:512]} | slice | bytes 1048576 | tf_op jit(solution)/shard_map/slice | solution.py:245
  13.0 1.0 %slice.71.top_ref = bf16[8,32,512]{2,1,0:T(8,128)(2,1)S(1)} slice(bf16[16,128,512]{2,1,0:T(8,128)(2,1)} %param.12), slice={[8:16], [40:72], [0:512]} | slice | bytes 524288 | tf_op jit(solution)/shard_map/slice | solution.py:269
  14.0 0.0 copy-start.6
  14.0 1.1 %slice.75.top_ref = bf16[8,48,512]{2,1,0:T(8,128)(2,1)S(1)} slice(bf16[16,128,512]{2,1,0:T(8,128)(2,1)} %param.12), slice={[8:16], [72:120], [0:512]} | slice | bytes 786432 | tf_op jit(solution)/shard_map/slice | solution.py:257
  15.1 1.7 %copy.16 = bf16[512,1536]{0,1:T(8,128)(2,1)S(1)} copy(bf16[512,1536]{1,0:T(8,128)(2,1)} %param.14) | data formatting | bytes 3145728 | tf_op args[2]
  16.8 0.0 copy-start.7
  16.8 0.0 copy-start.8
  16.9 0.0 copy-start.9
  16.9 0.0 copy-start.10
  16.9 0.0 copy-start.4
  16.9 0.0 copy-start.5
  17.0 0.1 pad_slice_fusion
  17.1 0.1 copy.17
  17.2 0.2 reshape.6.low_ref
  17.3 0.1 copy.18
  17.4 0.2 reshape.7.high_ref
  17.6 0.1 add_convert_fusion.edge_ref
  17.7 3.0 %bias.1 = (f32[16,256,256]{2,1,0:T(8,128)S(1)}, f32[16,256,256]{2,1,0:T(8,128)S(1)}) custom-call(s32[2]{0:T(128)S(1)} %add_convert_fusion.edge_ref, f32[16,512]{1,0:T(8,128)S(1)} %reshape.6.low_ref, f32[16,512]{1,0:T(8,128)S(1)} %reshape.7.high_ref), custom_call_target="tpu_custom_call" | custom-call | flops 4194304 | bytes 20971520 | tf_op jit(solution)/shard_map/bias/pallas_call | solution.py:90
  20.7 1.0 %fusion = (bf16[8,16,512]{2,1,0:T(8,128)(2,1)S(1)}, bf16[8,16,512]{2,1,0:T(8,128)(2,1)S(1)}) fusion(bf16[16,128,512]{2,1,0:T(8,128)(2,1)} %param.12), kind=kLoop, calls=%fused_computation.21 | loop fusion | bytes 524288 | tf_op jit(solution)/shard_map/slice | solution.py:269
  21.8 0.8 %pad_maximum_fusion.2.top_ref = bf16[8,16,512]{2,1,0:T(8,128)(2,1)S(1)} fusion(bf16[8,8,512]{2,1,0:T(8,128)(2,1)} %collective-permute-done, bf16[8,8,512]{2,1,0:T(8,128)(2,1)S(1)} %get-tuple-element.33), kind=kLoop, calls=%fused_computation.4 | loop fusion | flops 262144 | bytes 262144 | tf_op jit(solution)/shard_map/concatenate | solution.py:250
  22.6 0.8 %slice.80 = bf16[8,8,512]{2,1,0:T(8,128)(2,1)S(1)} slice(bf16[8,56,512]{2,1,0:T(8,128)(2,1)} %collective-permute-done.1), slice={[0:8], [48:56], [0:512]} | slice | bytes 131072 | tf_op jit(solution)/shard_map/slice | solution.py:251
  23.5 0.0 copy-start
  23.5 1.6 %copy-done = bf16[512,2048]{1,0:T(8,128)(2,1)S(1)} copy-done((bf16[512,2048]{1,0:T(8,128)(2,1)S(1)}, bf16[512,2048]{1,0:T(8,128)(2,1)}, u32[]{:S(2)}) %copy-start) | copy-done | bytes 2097176
  25.1 1.6 %copy-done.2 = bf16[2048,512]{1,0:T(8,128)(2,1)S(1)} copy-done((bf16[2048,512]{1,0:T(8,128)(2,1)S(1)}, bf16[2048,512]{1,0:T(8,128)(2,1)}, u32[]{:S(2)}) %copy-start.2) | copy-done | bytes 2097176
  26.7 4.8 %windows.5 = (bf16[8,16,512]{2,1,0:T(8,128)(2,1)S(1)}, bf16[8,16,512]{2,1,0:T(8,128)(2,1)S(1)}) custom-call(s32[1,8]{1,0:T(1,128)S(1)} %copy-done.5, f32[16]{0:T(128)S(1)} %exponential_multiply_fusion.scale_ref, bf16[8,16,512]{2,1,0:T(8,128)(2,1)S(1)} %pad_maximum_fusion.2.top_ref, bf16[8,16,512]{2,1,0:T(8,128)(2,1)S(1)} %pad_maximum_fusion.3.bottom_ref, ...), custom_call_target="tpu_custom_call" | custom-call | flops 7000000000 | bytes 4194304 | tf_op jit(solution)/shard_map/windows/pallas_call | solution.py:190
  31.5 1.5 %collective-permute-start.7 = (bf16[8,8,512]{2,1,0:T(8,128)(2,1)S(1)}, bf16[8,8,512]{2,1,0:T(8,128)(2,1)S(1)}, u32[]{:S(2)}, u32[]{:S(2)}) collective-permute-start(bf16[8,8,512]{2,1,0:T(8,128)(2,1)S(1)} %slice.78), channel_id=1, source_target_pairs={{0,1},{1,0},{2,3},{3,2},{4,5},{5,4},{6,7},{7,6},{8,9},{9,8},{10,11... | collective-permute-start | bytes 196616 | tf_op jit(solution)/shard_map/ppermute | solution.py:23
  33.1 1.0 %slice.84.bottom_ref = bf16[8,48,512]{2,1,0:T(8,128)(2,1)S(1)} slice(bf16[8,56,512]{2,1,0:T(8,128)(2,1)} %collective-permute-done.1), slice={[0:8], [0:48], [0:512]} | slice | bytes 786432 | tf_op jit(solution)/shard_map/slice | solution.py:257
  34.1 13.8 %windows.7 = (bf16[8,48,512]{2,1,0:T(8,128)(2,1)S(1)}, bf16[8,48,512]{2,1,0:T(8,128)(2,1)S(1)}) custom-call(s32[1,8]{1,0:T(1,128)S(1)} %copy-done.5, f32[16]{0:T(128)S(1)} %exponential_multiply_fusion.scale_ref, bf16[8,48,512]{2,1,0:T(8,128)(2,1)S(1)} %slice.75.top_ref, bf16[8,48,512]{2,1,0:T(8,128)(2,1)S(1)} %slice.84.bottom_ref, ...), custom_call_target="tpu_custom_call" | custom-call | flops 20999999488 | bytes 4194304 | tf_op jit(solution)/shard_map/windows/pallas_call | solution.py:190
  48.0 0.3 collective-permute-start.6
  48.3 1.0 %collective-permute-start.3 = (bf16[8,8,512]{2,1,0:T(8,128)(2,1)S(1)}, bf16[8,8,512]{2,1,0:T(8,128)(2,1)S(1)}, u32[]{:S(2)}, u32[]{:S(2)}) collective-permute-start(bf16[8,8,512]{2,1,0:T(8,128)(2,1)S(1)} %get-tuple-element.38), channel_id=1, source_target_pairs={{0,3},{1,2},{2,5},{3,4},{4,7},{5,6},{6,9},{7,8},{8,11},{9,10},{10,... | collective-permute-start | bytes 196616 | tf_op jit(solution)/shard_map/ppermute | solution.py:33
  49.4 1.0 %slice.82.bottom_ref = bf16[8,32,512]{2,1,0:T(8,128)(2,1)S(1)} slice(bf16[8,64,512]{2,1,0:T(8,128)(2,1)} %collective-permute-done.4), slice={[0:8], [32:64], [0:512]} | slice | bytes 524288 | tf_op jit(solution)/shard_map/slice | solution.py:270
  50.3 0.0 copy-start.3
  50.3 9.4 %windows.6 = (bf16[8,32,512]{2,1,0:T(8,128)(2,1)S(1)}, bf16[8,32,512]{2,1,0:T(8,128)(2,1)S(1)}) custom-call(s32[1,8]{1,0:T(1,128)S(1)} %copy-done.5, f32[16]{0:T(128)S(1)} %exponential_multiply_fusion.scale_ref, bf16[8,32,512]{2,1,0:T(8,128)(2,1)S(1)} %slice.71.top_ref, bf16[8,32,512]{2,1,0:T(8,128)(2,1)S(1)} %slice.82.bottom_ref, ...), custom_call_target="tpu_custom_call" | custom-call | flops 14000000000 | bytes 4194304 | tf_op jit(solution)/shard_map/windows/pallas_call | solution.py:190
  59.8 0.1 collective-permute-start.5
  59.9 1.0 %fusion.2 = (bf16[8,16,512]{2,1,0:T(8,128)(2,1)S(1)}, bf16[8,16,512]{2,1,0:T(8,128)(2,1)S(1)}) fusion(bf16[8,64,512]{2,1,0:T(8,128)(2,1)} %collective-permute-done.4), kind=kLoop, calls=%fused_computation.23 | loop fusion | bytes 524288 | tf_op jit(solution)/shard_map/slice | solution.py:270
  60.9 4.9 %windows.8 = (bf16[8,16,512]{2,1,0:T(8,128)(2,1)S(1)}, bf16[8,16,512]{2,1,0:T(8,128)(2,1)S(1)}) custom-call(s32[1,8]{1,0:T(1,128)S(1)} %copy-done.5, f32[16]{0:T(128)S(1)} %exponential_multiply_fusion.scale_ref, bf16[8,16,512]{2,1,0:T(8,128)(2,1)S(1)} %get-tuple-element.29.top_ref, bf16[8,16,512]{2,1,0:T(8,128)(2,1)S(1)} %get-tuple-element.34.bottom_ref, ...), custom_call_target="tpu_custom_call" | custom-call | flops 7000000000 | bytes 4194304 | tf_op jit(solution)/shard_map/windows/pallas_call | solution.py:190
  65.9 2.4 %collective-permute-done.5.refs_0_ = bf16[8,32,512]{2,1,0:T(8,128)(2,1)S(1)} collective-permute-done((bf16[8,32,512]{2,1,0:T(8,128)(2,1)S(1)}, bf16[8,32,512]{2,1,0:T(8,128)(2,1)S(1)}, u32[]{:S(2)}, u32[]{:S(2)}) %collective-permute-start.5) | collective-permute-done | bytes 262176 | tf_op jit(solution)/shard_map/ppermute | solution.py:23
  68.3 4.9 %windows.9 = (bf16[8,16,512]{2,1,0:T(8,128)(2,1)S(1)}, bf16[8,16,512]{2,1,0:T(8,128)(2,1)S(1)}) custom-call(s32[1,8]{1,0:T(1,128)S(1)} %copy-done.5, f32[16]{0:T(128)S(1)} %exponential_multiply_fusion.scale_ref, bf16[8,16,512]{2,1,0:T(8,128)(2,1)S(1)} %get-tuple-element.30.top_ref, bf16[8,16,512]{2,1,0:T(8,128)(2,1)S(1)} %get-tuple-element.35.bottom_ref, ...), custom_call_target="tpu_custom_call" | custom-call | flops 7000000000 | bytes 4194304 | tf_op jit(solution)/shard_map/windows/pallas_call | solution.py:190
  73.3 0.1 collective-permute-start.8
  73.4 0.1 collective-permute-start.9
  73.5 7.0 %collective-permute-done.8 = bf16[8,16,512]{2,1,0:T(8,128)(2,1)S(1)} collective-permute-done((bf16[8,16,512]{2,1,0:T(8,128)(2,1)S(1)}, bf16[8,16,512]{2,1,0:T(8,128)(2,1)S(1)}, u32[]{:S(2)}, u32[]{:S(2)}) %collective-permute-start.8) | collective-permute-done | bytes 131104 | tf_op jit(solution)/shard_map/ppermute | solution.py:23
  80.4 1.4 %collective-permute-done.9 = bf16[8,16,512]{2,1,0:T(8,128)(2,1)S(1)} collective-permute-done((bf16[8,16,512]{2,1,0:T(8,128)(2,1)S(1)}, bf16[8,16,512]{2,1,0:T(8,128)(2,1)S(1)}, u32[]{:S(2)}, u32[]{:S(2)}) %collective-permute-start.9) | collective-permute-done | bytes 131104 | tf_op jit(solution)/shard_map/ppermute | solution.py:23
  81.9 1.5 %pad_maximum_fusion = bf16[16,128,512]{2,1,0:T(8,128)(2,1)} fusion(bf16[8,128,512]{2,1,0:T(8,128)(2,1)S(1)} %slice_dynamic-update-slice_fusion, bf16[8,128,512]{2,1,0:T(8,128)(2,1)S(1)} %constant_dynamic-update-slice_fusion), kind=kLoop, calls=%fused_computation | loop fusion | flops 1048576 | bytes 4194304 | tf_op jit(solution)/shard_map/concatenate | solution.py:279
  (39 shorter events, 0.3 us)
Async XLA Ops:
  0.0 15.1 %copy-start.11 = (f32[16]{0:T(128)S(1)}, f32[16]{0:T(128)}, u32[]{:S(2)}) copy-start(f32[16]{0:T(128)} %param.18) | copy-start | bytes 196
  1.6 20.2 %collective-permute-start = (bf16[8,8,512]{2,1,0:T(8,128)(2,1)}, bf16[8,8,512]{2,1,0:T(8,128)(2,1)}, u32[]{:S(2)}, u32[]{:S(2)}) collective-permute-start(bf16[8,8,512]{2,1,0:T(8,128)(2,1)} %get-tuple-element.32), channel_id=1, source_target_pairs={{0,1},{1,0},{2,3},{3,2},{4,5},{5,4},{6,7},{7,6},{8,9},{9,8},{10,11... | collective-permute-start | bytes 196616 | tf_op jit(solution)/shard_map/ppermute | solution.py:23
  4.5 19.0 %collective-permute-start.2 = (bf16[8,8,512]{2,1,0:T(8,128)(2,1)S(1)}, bf16[8,8,512]{2,1,0:T(8,128)(2,1)S(1)}, u32[]{:S(2)}, u32[]{:S(2)}) collective-permute-start(bf16[8,8,512]{2,1,0:T(8,128)(2,1)S(1)} %get-tuple-element.31), channel_id=1, source_target_pairs={{0,31},{1,30},{2,1},{3,0},{4,3},{5,2},{6,5},{7,4},{8,7},{9,6},{10,... | collective-permute-start | bytes 196616 | tf_op jit(solution)/shard_map/ppermute | solution.py:33
  10.0 12.6 %collective-permute-start.1 = (bf16[8,56,512]{2,1,0:T(8,128)(2,1)}, bf16[8,56,512]{2,1,0:T(8,128)(2,1)}, u32[]{:S(2)}, u32[]{:S(2)}) collective-permute-start(bf16[8,56,512]{2,1,0:T(8,128)(2,1)} %slice.62), channel_id=1, source_target_pairs={{0,30},{2,0},{4,2},{6,4},{8,6},{10,8},{12,10},{14,12},{16,14},{18,... | collective-permute-start | bytes 1376264 | tf_op jit(solution)/shard_map/ppermute | solution.py:23
  13.0 36.3 %collective-permute-start.4 = (bf16[8,64,512]{2,1,0:T(8,128)(2,1)}, bf16[8,64,512]{2,1,0:T(8,128)(2,1)}, u32[]{:S(2)}, u32[]{:S(2)}) collective-permute-start(bf16[8,64,512]{2,1,0:T(8,128)(2,1)} %slice.69), channel_id=1, source_target_pairs={{0,30},{2,0},{4,2},{6,4},{8,6},{10,8},{12,10},{14,12},{16,14},{18,... | collective-permute-start | bytes 1572872 | tf_op jit(solution)/shard_map/ppermute | solution.py:23
  14.0 2.9 %copy-start.6 = (f32[16,31,31]{2,0,1:T(8,128)S(1)}, f32[16,31,31]{2,0,1:T(8,128)}, u32[]{:S(2)}) copy-start(f32[16,31,31]{2,0,1:T(8,128)} %param.19) | copy-start | bytes 184516
  16.8 4.9 %copy-start.7 = (f32[512]{0:T(512)S(1)}, f32[512]{0:T(512)}, u32[]{:S(2)}) copy-start(f32[512]{0:T(512)} %param.23) | copy-start | bytes 6148
  16.8 4.9 %copy-start.8 = (f32[512]{0:T(512)S(1)}, f32[512]{0:T(512)}, u32[]{:S(2)}) copy-start(f32[512]{0:T(512)} %param.22) | copy-start | bytes 6148
  16.9 4.9 %copy-start.9 = (f32[512]{0:T(512)S(1)}, f32[512]{0:T(512)}, u32[]{:S(2)}) copy-start(f32[512]{0:T(512)} %param.21) | copy-start | bytes 6148
  16.9 4.8 %copy-start.10 = (f32[512]{0:T(512)S(1)}, f32[512]{0:T(512)}, u32[]{:S(2)}) copy-start(f32[512]{0:T(512)} %param.20) | copy-start | bytes 6148
  16.9 6.6 %copy-start.4 = (bf16[512,512]{1,0:T(8,128)(2,1)S(1)}, bf16[512,512]{1,0:T(8,128)(2,1)}, u32[]{:S(2)}) copy-start(bf16[512,512]{1,0:T(8,128)(2,1)} %wproj_ref.9) | copy-start | bytes 1572868
  16.9 6.6 %copy-start.5 = (s32[1,8]{1,0:T(1,128)S(1)}, s32[1,8]{1,0:T(1,128)}, u32[]{:S(2)}) copy-start(s32[1,8]{1,0:T(1,128)} %tissue_ref.9) | copy-start | bytes 100
  23.5 1.6 %copy-start = (bf16[512,2048]{1,0:T(8,128)(2,1)S(1)}, bf16[512,2048]{1,0:T(8,128)(2,1)}, u32[]{:S(2)}) copy-start(bf16[512,2048]{1,0:T(8,128)(2,1)} %wfc1_ref.9) | copy-start | bytes 6291460
  25.1 1.6 %copy-start.2 = (bf16[2048,512]{1,0:T(8,128)(2,1)S(1)}, bf16[2048,512]{1,0:T(8,128)(2,1)}, u32[]{:S(2)}) copy-start(bf16[2048,512]{1,0:T(8,128)(2,1)} %wfc2_ref.9) | copy-start | bytes 6291460
  26.7 7.4 %copy-start.1 = (bf16[512,2048]{1,0:T(8,128)(2,1)S(1)}, bf16[512,2048]{1,0:T(8,128)(2,1)}, u32[]{:S(2)}) copy-start(bf16[512,2048]{1,0:T(8,128)(2,1)} %wfc1_ref.9) | copy-start | bytes 6291460
  31.5 28.4 %collective-permute-start.7 = (bf16[8,8,512]{2,1,0:T(8,128)(2,1)S(1)}, bf16[8,8,512]{2,1,0:T(8,128)(2,1)S(1)}, u32[]{:S(2)}, u32[]{:S(2)}) collective-permute-start(bf16[8,8,512]{2,1,0:T(8,128)(2,1)S(1)} %slice.78), channel_id=1, source_target_pairs={{0,1},{1,0},{2,3},{3,2},{4,5},{5,4},{6,7},{7,6},{8,9},{9,8},{10,11... | collective-permute-start | bytes 196616 | tf_op jit(solution)/shard_map/ppermute | solution.py:23
  48.0 12.9 %collective-permute-start.6 = (bf16[8,56,512]{2,1,0:T(8,128)(2,1)S(1)}, bf16[8,56,512]{2,1,0:T(8,128)(2,1)S(1)}, u32[]{:S(2)}, u32[]{:S(2)}) collective-permute-start(bf16[8,56,512]{2,1,0:T(8,128)(2,1)S(1)} %pad_maximum_fusion.1), channel_id=1, source_target_pairs={{0,2},{2,4},{4,6},{6,8},{8,10},{10,12},{12,14},{14,16},{16,18},{18... | collective-permute-start | bytes 1376264 | tf_op jit(solution)/shard_map/ppermute | solution.py:23
  48.3 11.6 %collective-permute-start.3 = (bf16[8,8,512]{2,1,0:T(8,128)(2,1)S(1)}, bf16[8,8,512]{2,1,0:T(8,128)(2,1)S(1)}, u32[]{:S(2)}, u32[]{:S(2)}) collective-permute-start(bf16[8,8,512]{2,1,0:T(8,128)(2,1)S(1)} %get-tuple-element.38), channel_id=1, source_target_pairs={{0,3},{1,2},{2,5},{3,4},{4,7},{5,6},{6,9},{7,8},{8,11},{9,10},{10,... | collective-permute-start | bytes 196616 | tf_op jit(solution)/shard_map/ppermute | solution.py:33
  50.3 10.6 %copy-start.3 = (bf16[2048,512]{1,0:T(8,128)(2,1)S(1)}, bf16[2048,512]{1,0:T(8,128)(2,1)}, u32[]{:S(2)}) copy-start(bf16[2048,512]{1,0:T(8,128)(2,1)} %wfc2_ref.9) | copy-start | bytes 6291460
  59.8 8.5 %collective-permute-start.5 = (bf16[8,32,512]{2,1,0:T(8,128)(2,1)S(1)}, bf16[8,32,512]{2,1,0:T(8,128)(2,1)S(1)}, u32[]{:S(2)}, u32[]{:S(2)}) collective-permute-start(bf16[8,32,512]{2,1,0:T(8,128)(2,1)S(1)} %get-tuple-element.20), channel_id=1, source_target_pairs={{0,2},{2,4},{4,6},{6,8},{8,10},{10,12},{12,14},{14,16},{16,18},{18... | collective-permute-start | bytes 786440 | tf_op jit(solution)/shard_map/ppermute | solution.py:23
  73.3 7.1 %collective-permute-start.8 = (bf16[8,16,512]{2,1,0:T(8,128)(2,1)S(1)}, bf16[8,16,512]{2,1,0:T(8,128)(2,1)S(1)}, u32[]{:S(2)}, u32[]{:S(2)}) collective-permute-start(bf16[8,16,512]{2,1,0:T(8,128)(2,1)S(1)} %get-tuple-element.25), channel_id=1, source_target_pairs={{0,2},{2,4},{4,6},{6,8},{8,10},{10,12},{12,14},{14,16},{16,18},{18... | collective-permute-start | bytes 393224 | tf_op jit(solution)/shard_map/ppermute | solution.py:23
  73.4 8.5 %collective-permute-start.9 = (bf16[8,16,512]{2,1,0:T(8,128)(2,1)S(1)}, bf16[8,16,512]{2,1,0:T(8,128)(2,1)S(1)}, u32[]{:S(2)}, u32[]{:S(2)}) collective-permute-start(bf16[8,16,512]{2,1,0:T(8,128)(2,1)S(1)} %get-tuple-element.26), channel_id=1, source_target_pairs={{0,2},{2,4},{4,6},{6,8},{8,10},{10,12},{12,14},{14,16},{16,18},{18... | collective-permute-start | bytes 393224 | tf_op jit(solution)/shard_map/ppermute | solution.py:23

commit v5 on v4

--- a/solution.py
+++ b/solution.py
@@ -259,7 +259,7 @@
     above_right = shifted(
         jnp.concatenate([bottom_right, bottom_end[:, :SHIFT]], axis=1), "row", 1
     )
-    cuts = [windows // 2, windows // 4, windows // 8, 0]
+    cuts = [windows // 2, windows // 4, 0]
     sent = [(above_right, from_left, from_corner)]
     own, above = ([top_right, top_end[:, :SHIFT]], [above_right])
     for step, (hi, lo) in enumerate(zip(cuts, cuts[1:])):

time: 84 us -> 84.4 us (level)
  waiting for transfers between devices: 10.8 us -> 8.39 us
  other arithmetic: 2.52 us -> 4.68 us
  local copies, waits for them, and re-layouts: 17.9 us -> 19.3 us
    ppermute x8 -> x7, waiting for transfers between devices: 10.8 us -> 8.39 us  [shifted(): return lax.ppermute(x, axis, [(i, (i + by) % count) for i in range(count)])]
    reshape x1, local copies, waits for them, and re-layouts: 0.15 us -> 1.1 us  [build_bias(): high = table[:, :, WIN:].reshape(HEADS, SPAN)]
    reshape x1, local copies, waits for them, and re-layouts: 0.15 us -> 1.1 us  [build_bias(): low = table[:, :, :WIN].reshape(HEADS, SPAN)]
    slice x2 -> x1, local copies, waits for them, and re-layouts: 1.96 us -> 1.06 us  [on_device(): crop[SHIFT:, start + SHIFT:stop + SHIFT]]
    slice x2 -> x1, local copies, waits for them, and re-layouts: 1.96 us -> 1.07 us  [on_device(): below_left[:, start:stop]]
    pallas_call x5 -> x4, Pallas kernels: 37.9 us -> 37.2 us  [run_windows(): pl.pallas_call(functools.partial(window_kernel, first, len(after)), grid=...]
    ppermute x8 -> x7, starting transfers between devices: 6.15 us -> 6.13 us  [shifted(): return lax.ppermute(x, axis, [(i, (i + by) % count) for i in range(count)])]
    unnamed x34 -> x23, local copies, waits for them, and re-layouts: 5.07 us -> 5.06 us
  transfers between devices with their start and end apart: 10 -> 9, of which waited for: 3 -> 1; matrix products, arithmetic and copies ran while one was open for 17% -> 21% of each run, Pallas kernels for 43% -> 48%
where the time goes in v5:
time: 84.4 us; the launch traced here: 83.7 us
  Pallas kernels  40.2 us (48%)
  local copies, waits for them, and re-layouts  19.3 us (23%)
  starting transfers between devices  10.9 us (13%)
  waiting for transfers between devices  8.39 us (10%)
  other arithmetic  4.68 us (6%)
    pallas_call x4, Pallas kernels, run_windows(): pl.pallas_call(functools.partial(window_kernel, first, len(after)), grid=...  37.2 us
    ppermute x7, waiting for transfers between devices, shifted(): return lax.ppermute(x, axis, [(i, (i + by) % count) for i in range(count)])  8.39 us
    ppermute x7, starting transfers between devices, shifted(): return lax.ppermute(x, axis, [(i, (i + by) % count) for i in range(count)])  6.13 us
    unnamed x23, local copies, waits for them, and re-layouts  5.06 us
    ppermute x2, starting transfers between devices, shifted_both(): return lax.ppermute(x, ('row', 'col'), pairs)  4.74 us
    pallas_call x1, Pallas kernels, build_bias(): pl.pallas_call(bias_kernel, out_shape=[jax.ShapeDtypeStruct((HEADS, TOKEN...  3.01 us
    slice x1, local copies, waits for them, and re-layouts, on_device(): below_left = shifted(crop[:SHIFT, SHIFT:split], 'row', -1)  1.87 us
    slice x1, local copies, waits for them, and re-layouts, on_device(): below_right = shifted(crop[:SHIFT, split:], 'row', -1)  1.83 us
  transfers between devices with their start and end apart: 9, of which 1 were waited for; matrix products, arithmetic and copies ran while one was open for 21% of the time, Pallas kernels for 48%

profile of v5, /device:TPU:0, one launch (start us, length us, event | category | flops | bytes accessed | tf_op | source)
XLA Modules:
  0.0 83.7 jit_solution(17295850868628854269)
XLA Ops:
  0.0 1.6 %fusion.1 = (bf16[8,8,512]{2,1,0:T(8,128)(2,1)}, bf16[8,8,512]{2,1,0:T(8,128)(2,1)}, bf16[8,8,512]{2,1,0:T(8,128)(2,1)}) fusion(bf16[16,128,512]{2,1,0:T(8,128)(2,1)} %param.12), kind=kLoop, calls=%fused_computation.16 | loop fusion | bytes 393216 | tf_op jit(solution)/shard_map/slice | solution.py:242
  1.6 2.9 %collective-permute-start = (bf16[8,8,512]{2,1,0:T(8,128)(2,1)}, bf16[8,8,512]{2,1,0:T(8,128)(2,1)}, u32[]{:S(2)}, u32[]{:S(2)}) collective-permute-start(bf16[8,8,512]{2,1,0:T(8,128)(2,1)} %get-tuple-element.28), channel_id=1, source_target_pairs={{0,1},{1,0},{2,3},{3,2},{4,5},{5,4},{6,7},{7,6},{8,9},{9,8},{10,11... | collective-permute-start | bytes 196616 | tf_op jit(solution)/shard_map/ppermute | solution.py:23
  4.6 3.7 %collective-permute-start.2 = (bf16[8,8,512]{2,1,0:T(8,128)(2,1)}, bf16[8,8,512]{2,1,0:T(8,128)(2,1)}, u32[]{:S(2)}, u32[]{:S(2)}) collective-permute-start(bf16[8,8,512]{2,1,0:T(8,128)(2,1)} %get-tuple-element.27), channel_id=1, source_target_pairs={{0,31},{1,30},{2,1},{3,0},{4,3},{5,2},{6,5},{7,4},{8,7},{9,6},{10,... | collective-permute-start | bytes 196616 | tf_op jit(solution)/shard_map/ppermute | solution.py:33
  8.3 1.8 %slice.56 = bf16[8,56,512]{2,1,0:T(8,128)(2,1)} slice(bf16[16,128,512]{2,1,0:T(8,128)(2,1)} %param.12), slice={[0:8], [72:128], [0:512]} | slice | bytes 917504 | tf_op jit(solution)/shard_map/slice | solution.py:244
  10.1 1.1 %collective-permute-start.1 = (bf16[8,56,512]{2,1,0:T(8,128)(2,1)}, bf16[8,56,512]{2,1,0:T(8,128)(2,1)}, u32[]{:S(2)}, u32[]{:S(2)}) collective-permute-start(bf16[8,56,512]{2,1,0:T(8,128)(2,1)} %slice.56), channel_id=1, source_target_pairs={{0,30},{2,0},{4,2},{6,4},{8,6},{10,8},{12,10},{14,12},{16,14},{18,... | collective-permute-start | bytes 1376264 | tf_op jit(solution)/shard_map/ppermute | solution.py:23
  11.2 1.9 %slice.63 = bf16[8,64,512]{2,1,0:T(8,128)(2,1)} slice(bf16[16,128,512]{2,1,0:T(8,128)(2,1)} %param.12), slice={[0:8], [8:72], [0:512]} | slice | bytes 1048576 | tf_op jit(solution)/shard_map/slice | solution.py:245
  13.1 0.0 collective-permute-start.4
  13.1 1.1 %fusion = (bf16[8,32,512]{2,1,0:T(8,128)(2,1)S(1)}, bf16[8,32,512]{2,1,0:T(8,128)(2,1)S(1)}) fusion(bf16[16,128,512]{2,1,0:T(8,128)(2,1)} %param.12), kind=kLoop, calls=%fused_computation.15 | loop fusion | bytes 1048576 | tf_op jit(solution)/shard_map/slice | solution.py:269
  14.2 0.1 pad_slice_fusion
  14.3 0.1 add_convert_fusion.edge_ref
  14.4 1.0 %slice.65.top_ref = bf16[8,48,512]{2,1,0:T(8,128)(2,1)S(1)} slice(bf16[16,128,512]{2,1,0:T(8,128)(2,1)} %param.12), slice={[8:16], [72:120], [0:512]} | slice | bytes 786432 | tf_op jit(solution)/shard_map/slice | solution.py:257
  15.5 0.0 copy-start.7
  15.5 0.0 copy-start.8
  15.5 0.0 copy-start.4
  15.5 0.0 copy-start.5
  15.5 1.8 %copy.16 = bf16[512,1536]{0,1:T(8,128)(2,1)S(1)} copy(bf16[512,1536]{1,0:T(8,128)(2,1)} %param.14) | data formatting | bytes 3145728 | tf_op args[2]
  17.3 0.8 copy.17
  18.1 1.1 %reshape.6.low_ref = f32[16,512]{1,0:T(8,128)S(1)} reshape(f32[16,32,16]{2,1,0:T(8,128)} %copy.17) | data formatting | bytes 65536 | tf_op jit(solution)/shard_map/reshape | solution.py:88
  19.2 0.8 copy.18
  20.0 1.1 %reshape.7.high_ref = f32[16,512]{1,0:T(8,128)S(1)} reshape(f32[16,32,16]{2,1,0:T(8,128)} %copy.18) | data formatting | bytes 65536 | tf_op jit(solution)/shard_map/reshape | solution.py:89
  21.1 3.0 %bias.1 = (f32[16,256,256]{2,1,0:T(8,128)S(1)}, f32[16,256,256]{2,1,0:T(8,128)S(1)}) custom-call(s32[2]{0:T(128)S(1)} %add_convert_fusion.edge_ref, f32[16,512]{1,0:T(8,128)S(1)} %reshape.6.low_ref, f32[16,512]{1,0:T(8,128)S(1)} %reshape.7.high_ref), custom_call_target="tpu_custom_call" | custom-call | flops 4194304 | bytes 20971520 | tf_op jit(solution)/shard_map/bias/pallas_call | solution.py:90
  24.1 0.7 exponential_multiply_fusion.scale_ref
  24.7 0.7 pad_maximum_fusion.4.norm_ref
  25.5 0.0 collective-permute-done
  25.5 0.9 %pad_maximum_fusion.2.top_ref = bf16[8,16,512]{2,1,0:T(8,128)(2,1)S(1)} fusion(bf16[8,8,512]{2,1,0:T(8,128)(2,1)} %collective-permute-done, bf16[8,8,512]{2,1,0:T(8,128)(2,1)} %get-tuple-element.29), kind=kLoop, calls=%fused_computation.4 | loop fusion | flops 262144 | bytes 262144 | tf_op jit(solution)/shard_map/concatenate | solution.py:250
  26.4 0.0 collective-permute-done.1
  26.4 0.8 %slice.72 = bf16[8,8,512]{2,1,0:T(8,128)(2,1)S(1)} slice(bf16[8,56,512]{2,1,0:T(8,128)(2,1)} %collective-permute-done.1), slice={[0:8], [48:56], [0:512]} | slice | bytes 131072 | tf_op jit(solution)/shard_map/slice | solution.py:251
  27.2 0.8 %pad_maximum_fusion.3.bottom_ref = bf16[8,16,512]{2,1,0:T(8,128)(2,1)S(1)} fusion(bf16[8,8,512]{2,1,0:T(8,128)(2,1)} %collective-permute-done.2, bf16[8,8,512]{2,1,0:T(8,128)(2,1)S(1)} %slice.72), kind=kLoop, calls=%fused_computation.5 | loop fusion | flops 262144 | bytes 262144 | tf_op jit(solution)/shard_map/concatenate | solution.py:251
  28.1 0.0 copy-start
  28.1 1.6 %copy-done = bf16[512,2048]{1,0:T(8,128)(2,1)S(1)} copy-done((bf16[512,2048]{1,0:T(8,128)(2,1)S(1)}, bf16[512,2048]{1,0:T(8,128)(2,1)}, u32[]{:S(2)}) %copy-start) | copy-done | bytes 2097176
  29.7 1.6 %copy-done.2 = bf16[2048,512]{1,0:T(8,128)(2,1)S(1)} copy-done((bf16[2048,512]{1,0:T(8,128)(2,1)S(1)}, bf16[2048,512]{1,0:T(8,128)(2,1)}, u32[]{:S(2)}) %copy-start.2) | copy-done | bytes 2097176
  31.3 4.9 %windows.4 = (bf16[8,16,512]{2,1,0:T(8,128)(2,1)S(1)}, bf16[8,16,512]{2,1,0:T(8,128)(2,1)S(1)}) custom-call(s32[1,8]{1,0:T(1,128)S(1)} %copy-done.5, f32[16]{0:T(128)S(1)} %exponential_multiply_fusion.scale_ref, bf16[8,16,512]{2,1,0:T(8,128)(2,1)S(1)} %pad_maximum_fusion.2.top_ref, bf16[8,16,512]{2,1,0:T(8,128)(2,1)S(1)} %pad_maximum_fusion.3.bottom_ref, ...), custom_call_target="tpu_custom_call" | custom-call | flops 7000000000 | bytes 4194304 | tf_op jit(solution)/shard_map/windows/pallas_call | solution.py:190
  36.2 1.6 %collective-permute-start.6 = (bf16[8,8,512]{2,1,0:T(8,128)(2,1)S(1)}, bf16[8,8,512]{2,1,0:T(8,128)(2,1)S(1)}, u32[]{:S(2)}, u32[]{:S(2)}) collective-permute-start(bf16[8,8,512]{2,1,0:T(8,128)(2,1)S(1)} %slice.68), channel_id=1, source_target_pairs={{0,1},{1,0},{2,3},{3,2},{4,5},{5,4},{6,7},{7,6},{8,9},{9,8},{10,11... | collective-permute-start | bytes 196616 | tf_op jit(solution)/shard_map/ppermute | solution.py:23
  37.8 1.0 %slice.74.bottom_ref = bf16[8,48,512]{2,1,0:T(8,128)(2,1)S(1)} slice(bf16[8,56,512]{2,1,0:T(8,128)(2,1)} %collective-permute-done.1), slice={[0:8], [0:48], [0:512]} | slice | bytes 786432 | tf_op jit(solution)/shard_map/slice | solution.py:257
  38.8 13.6 %windows.5 = (bf16[8,48,512]{2,1,0:T(8,128)(2,1)S(1)}, bf16[8,48,512]{2,1,0:T(8,128)(2,1)S(1)}) custom-call(s32[1,8]{1,0:T(1,128)S(1)} %copy-done.5, f32[16]{0:T(128)S(1)} %exponential_multiply_fusion.scale_ref, bf16[8,48,512]{2,1,0:T(8,128)(2,1)S(1)} %slice.65.top_ref, bf16[8,48,512]{2,1,0:T(8,128)(2,1)S(1)} %slice.74.bottom_ref, ...), custom_call_target="tpu_custom_call" | custom-call | flops 20999999488 | bytes 4194304 | tf_op jit(solution)/shard_map/windows/pallas_call | solution.py:190
  52.6 0.3 collective-permute-start.5
  52.8 1.0 %collective-permute-start.3 = (bf16[8,8,512]{2,1,0:T(8,128)(2,1)S(1)}, bf16[8,8,512]{2,1,0:T(8,128)(2,1)S(1)}, u32[]{:S(2)}, u32[]{:S(2)}) collective-permute-start(bf16[8,8,512]{2,1,0:T(8,128)(2,1)S(1)} %get-tuple-element.34), channel_id=1, source_target_pairs={{0,3},{1,2},{2,5},{3,4},{4,7},{5,6},{6,9},{7,8},{8,11},{9,10},{10,... | collective-permute-start | bytes 196616 | tf_op jit(solution)/shard_map/ppermute | solution.py:33
  53.9 0.0 collective-permute-done.4
  53.9 1.1 %fusion.2 = (bf16[8,32,512]{2,1,0:T(8,128)(2,1)S(1)}, bf16[8,32,512]{2,1,0:T(8,128)(2,1)S(1)}) fusion(bf16[8,64,512]{2,1,0:T(8,128)(2,1)} %collective-permute-done.4), kind=kLoop, calls=%fused_computation.17 | loop fusion | bytes 1048576 | tf_op jit(solution)/shard_map/slice | solution.py:270
  54.9 0.0 copy-start.3
  55.0 9.3 %windows.6 = (bf16[8,32,512]{2,1,0:T(8,128)(2,1)S(1)}, bf16[8,32,512]{2,1,0:T(8,128)(2,1)S(1)}) custom-call(s32[1,8]{1,0:T(1,128)S(1)} %copy-done.5, f32[16]{0:T(128)S(1)} %exponential_multiply_fusion.scale_ref, bf16[8,32,512]{2,1,0:T(8,128)(2,1)S(1)} %get-tuple-element.25.top_ref, bf16[8,32,512]{2,1,0:T(8,128)(2,1)S(1)} %get-tuple-element.30.bottom_ref, ...), custom_call_target="tpu_custom_call" | custom-call | flops 14000000000 | bytes 4194304 | tf_op jit(solution)/shard_map/windows/pallas_call | solution.py:190
  64.3 0.1 collective-permute-start.8
  64.4 0.0 collective-permute-done.3.refs_2_
  64.4 9.3 %windows.7 = (bf16[8,32,512]{2,1,0:T(8,128)(2,1)S(1)}, bf16[8,32,512]{2,1,0:T(8,128)(2,1)S(1)}) custom-call(s32[1,8]{1,0:T(1,128)S(1)} %copy-done.5, f32[16]{0:T(128)S(1)} %exponential_multiply_fusion.scale_ref, bf16[8,32,512]{2,1,0:T(8,128)(2,1)S(1)} %get-tuple-element.26.top_ref, bf16[8,32,512]{2,1,0:T(8,128)(2,1)S(1)} %get-tuple-element.31.bottom_ref, ...), custom_call_target="tpu_custom_call" | custom-call | flops 14000000000 | bytes 4194304 | tf_op jit(solution)/shard_map/windows/pallas_call | solution.py:190
  73.8 0.1 collective-permute-start.7
  73.9 0.0 collective-permute-done.8
  73.9 8.4 %collective-permute-done.7 = bf16[8,32,512]{2,1,0:T(8,128)(2,1)S(1)} collective-permute-done((bf16[8,32,512]{2,1,0:T(8,128)(2,1)S(1)}, bf16[8,32,512]{2,1,0:T(8,128)(2,1)S(1)}, u32[]{:S(2)}, u32[]{:S(2)}) %collective-permute-start.7) | collective-permute-done | bytes 262176 | tf_op jit(solution)/shard_map/ppermute | solution.py:23
  82.3 1.4 %pad_maximum_fusion = bf16[16,128,512]{2,1,0:T(8,128)(2,1)} fusion(bf16[8,128,512]{2,1,0:T(8,128)(2,1)S(1)} %slice_dynamic-update-slice_fusion, bf16[8,56,512]{2,1,0:T(8,128)(2,1)S(1)} %collective-permute-done.5.refs_0_, bf16[8,32,512]{2,1,0:T(8,128)(2,1)S(1)} %collective-permute-done.8, bf16[8,32,512]{2,1,0:T(8,128)(2,1)S(1)} %collective-permute-done.7, ...), kind=kLoop, calls=%fused_computation | loop fusion | flops 10485760 | bytes 4194304 | tf_op jit(solution)/shard_map/concatenate | solution.py:279
  (22 shorter events, 0.2 us)
Async XLA Ops:
  0.0 14.2 %copy-start.6 = (f32[16,31,31]{2,0,1:T(8,128)S(1)}, f32[16,31,31]{2,0,1:T(8,128)}, u32[]{:S(2)}) copy-start(f32[16,31,31]{2,0,1:T(8,128)} %param.19) | copy-start | bytes 184516
  1.6 23.8 %collective-permute-start = (bf16[8,8,512]{2,1,0:T(8,128)(2,1)}, bf16[8,8,512]{2,1,0:T(8,128)(2,1)}, u32[]{:S(2)}, u32[]{:S(2)}) collective-permute-start(bf16[8,8,512]{2,1,0:T(8,128)(2,1)} %get-tuple-element.28), channel_id=1, source_target_pairs={{0,1},{1,0},{2,3},{3,2},{4,5},{5,4},{6,7},{7,6},{8,9},{9,8},{10,11... | collective-permute-start | bytes 196616 | tf_op jit(solution)/shard_map/ppermute | solution.py:23
  4.6 22.6 %collective-permute-start.2 = (bf16[8,8,512]{2,1,0:T(8,128)(2,1)}, bf16[8,8,512]{2,1,0:T(8,128)(2,1)}, u32[]{:S(2)}, u32[]{:S(2)}) collective-permute-start(bf16[8,8,512]{2,1,0:T(8,128)(2,1)} %get-tuple-element.27), channel_id=1, source_target_pairs={{0,31},{1,30},{2,1},{3,0},{4,3},{5,2},{6,5},{7,4},{8,7},{9,6},{10,... | collective-permute-start | bytes 196616 | tf_op jit(solution)/shard_map/ppermute | solution.py:33
  10.1 16.3 %collective-permute-start.1 = (bf16[8,56,512]{2,1,0:T(8,128)(2,1)}, bf16[8,56,512]{2,1,0:T(8,128)(2,1)}, u32[]{:S(2)}, u32[]{:S(2)}) collective-permute-start(bf16[8,56,512]{2,1,0:T(8,128)(2,1)} %slice.56), channel_id=1, source_target_pairs={{0,30},{2,0},{4,2},{6,4},{8,6},{10,8},{12,10},{14,12},{16,14},{18,... | collective-permute-start | bytes 1376264 | tf_op jit(solution)/shard_map/ppermute | solution.py:23
  13.1 40.8 %collective-permute-start.4 = (bf16[8,64,512]{2,1,0:T(8,128)(2,1)}, bf16[8,64,512]{2,1,0:T(8,128)(2,1)}, u32[]{:S(2)}, u32[]{:S(2)}) collective-permute-start(bf16[8,64,512]{2,1,0:T(8,128)(2,1)} %slice.63), channel_id=1, source_target_pairs={{0,30},{2,0},{4,2},{6,4},{8,6},{10,8},{12,10},{14,12},{16,14},{18,... | collective-permute-start | bytes 1572872 | tf_op jit(solution)/shard_map/ppermute | solution.py:23
  15.5 9.3 %copy-start.7 = (f32[512]{0:T(512)S(1)}, f32[512]{0:T(512)}, u32[]{:S(2)}) copy-start(f32[512]{0:T(512)} %param.23) | copy-start | bytes 6148
  15.5 9.3 %copy-start.8 = (f32[512]{0:T(512)S(1)}, f32[512]{0:T(512)}, u32[]{:S(2)}) copy-start(f32[512]{0:T(512)} %param.22) | copy-start | bytes 6148
  15.5 12.6 %copy-start.4 = (bf16[512,512]{1,0:T(8,128)(2,1)S(1)}, bf16[512,512]{1,0:T(8,128)(2,1)}, u32[]{:S(2)}) copy-start(bf16[512,512]{1,0:T(8,128)(2,1)} %wproj_ref.7) | copy-start | bytes 1572868
  15.5 12.6 %copy-start.5 = (s32[1,8]{1,0:T(1,128)S(1)}, s32[1,8]{1,0:T(1,128)}, u32[]{:S(2)}) copy-start(s32[1,8]{1,0:T(1,128)} %tissue_ref.7) | copy-start | bytes 100
  28.1 1.6 %copy-start = (bf16[512,2048]{1,0:T(8,128)(2,1)S(1)}, bf16[512,2048]{1,0:T(8,128)(2,1)}, u32[]{:S(2)}) copy-start(bf16[512,2048]{1,0:T(8,128)(2,1)} %wfc1_ref.7) | copy-start | bytes 6291460
  29.7 1.6 %copy-start.2 = (bf16[2048,512]{1,0:T(8,128)(2,1)S(1)}, bf16[2048,512]{1,0:T(8,128)(2,1)}, u32[]{:S(2)}) copy-start(bf16[2048,512]{1,0:T(8,128)(2,1)} %wfc2_ref.7) | copy-start | bytes 6291460
  31.3 7.5 %copy-start.1 = (bf16[512,2048]{1,0:T(8,128)(2,1)S(1)}, bf16[512,2048]{1,0:T(8,128)(2,1)}, u32[]{:S(2)}) copy-start(bf16[512,2048]{1,0:T(8,128)(2,1)} %wfc1_ref.7) | copy-start | bytes 6291460
  36.2 28.1 %collective-permute-start.6 = (bf16[8,8,512]{2,1,0:T(8,128)(2,1)S(1)}, bf16[8,8,512]{2,1,0:T(8,128)(2,1)S(1)}, u32[]{:S(2)}, u32[]{:S(2)}) collective-permute-start(bf16[8,8,512]{2,1,0:T(8,128)(2,1)S(1)} %slice.68), channel_id=1, source_target_pairs={{0,1},{1,0},{2,3},{3,2},{4,5},{5,4},{6,7},{7,6},{8,9},{9,8},{10,11... | collective-permute-start | bytes 196616 | tf_op jit(solution)/shard_map/ppermute | solution.py:23
  52.6 11.8 %collective-permute-start.5 = (bf16[8,56,512]{2,1,0:T(8,128)(2,1)S(1)}, bf16[8,56,512]{2,1,0:T(8,128)(2,1)S(1)}, u32[]{:S(2)}, u32[]{:S(2)}) collective-permute-start(bf16[8,56,512]{2,1,0:T(8,128)(2,1)S(1)} %pad_maximum_fusion.1), channel_id=1, source_target_pairs={{0,2},{2,4},{4,6},{6,8},{8,10},{10,12},{12,14},{14,16},{16,18},{18... | collective-permute-start | bytes 1376264 | tf_op jit(solution)/shard_map/ppermute | solution.py:23
  52.8 11.6 %collective-permute-start.3 = (bf16[8,8,512]{2,1,0:T(8,128)(2,1)S(1)}, bf16[8,8,512]{2,1,0:T(8,128)(2,1)S(1)}, u32[]{:S(2)}, u32[]{:S(2)}) collective-permute-start(bf16[8,8,512]{2,1,0:T(8,128)(2,1)S(1)} %get-tuple-element.34), channel_id=1, source_target_pairs={{0,3},{1,2},{2,5},{3,4},{4,7},{5,6},{6,9},{7,8},{8,11},{9,10},{10,... | collective-permute-start | bytes 196616 | tf_op jit(solution)/shard_map/ppermute | solution.py:33
  54.9 9.5 %copy-start.3 = (bf16[2048,512]{1,0:T(8,128)(2,1)S(1)}, bf16[2048,512]{1,0:T(8,128)(2,1)}, u32[]{:S(2)}) copy-start(bf16[2048,512]{1,0:T(8,128)(2,1)} %wfc2_ref.7) | copy-start | bytes 6291460
  64.3 9.7 %collective-permute-start.8 = (bf16[8,32,512]{2,1,0:T(8,128)(2,1)S(1)}, bf16[8,32,512]{2,1,0:T(8,128)(2,1)S(1)}, u32[]{:S(2)}, u32[]{:S(2)}) collective-permute-start(bf16[8,32,512]{2,1,0:T(8,128)(2,1)S(1)} %get-tuple-element.22), channel_id=1, source_target_pairs={{0,2},{2,4},{4,6},{6,8},{8,10},{10,12},{12,14},{14,16},{16,18},{18... | collective-permute-start | bytes 786440 | tf_op jit(solution)/shard_map/ppermute | solution.py:23
  73.8 8.5 %collective-permute-start.7 = (bf16[8,32,512]{2,1,0:T(8,128)(2,1)S(1)}, bf16[8,32,512]{2,1,0:T(8,128)(2,1)S(1)}, u32[]{:S(2)}, u32[]{:S(2)}) collective-permute-start(bf16[8,32,512]{2,1,0:T(8,128)(2,1)S(1)} %get-tuple-element.21), channel_id=1, source_target_pairs={{0,2},{2,4},{4,6},{6,8},{8,10},{10,12},{12,14},{14,16},{16,18},{18... | collective-permute-start | bytes 786440 | tf_op jit(solution)/shard_map/ppermute | solution.py:23
